TPU v7x, 128 devices: a whole 4x4x4 slice. The times are simulated.
128 devices in a mesh: ep: 128 (over y, z, x, core).
Axes of the slice: x: 4, y: 4, z: 4, core: 2. Of those that a mesh axis runs over, the one named last changes fastest.
Arguments:
- queries: bfloat16 [1, 2048, 64, 576], P(None, 'ep'), may hold values from -320 to 320
- latent_cache: bfloat16 [2048, 128, 576], P('ep'), may hold values from -4 to 4
- new_latent: bfloat16 [1, 2048, 576], P(None, 'ep'), may hold values from -4 to 4
- lengths: int32 [2048], P('ep'), may hold values from 16 to 128
- hidden: bfloat16 [1, 2048, 3584], P(None, 'ep'), may hold values from -400 to 400
- norm_gain: float32 [3584], replicated, may hold values from 0.1 to 1.9
- routes: int32 [1, 2048, 8], P(None, 'ep'), may hold values from 0 to 127, all different within a row; in each aligned block of 16 rows (0 to 15, 16 to 31, ..., all dimensions but the last counted through in order) at most 3 rows name the same one
- route_weight: float32 [1, 2048, 8], P(None, 'ep'), may hold values from 0.1 to 1
- gate_weight: bfloat16 [128, 3584, 1024], P('ep'), may hold values from -0.09375 to 0.09375
- up_weight: bfloat16 [128, 3584, 1024], P('ep'), may hold values from -0.09375 to 0.09375
- down_weight: bfloat16 [128, 1024, 3584], P('ep'), may hold values from -0.1875 to 0.1875
Outputs:
- attended: bfloat16 [1, 2048, 64, 512], P(None, 'ep')
- expert_mix: bfloat16 [1, 2048, 3584], P(None, 'ep')
Inputs may be any that keep to these rules, and one draw needn't show every extreme that they name: `routes`: each token names 8 different experts; among the rows of one device in one step no expert is named more than 3 times.
All inputs are finite; a program needn't handle non-finite values.
Results may differ from a plain program's by a relative error of at most 0.0071.
Values may be sent and summed in bfloat16 or wider, within the bound.
A program may use at most 128 MiB of HBM per device.

v0:
```python
import jax
import jax.numpy as jnp
from jax import lax
from jax.sharding import PartitionSpec as P

LAT = 512
TOPK = 8


soft_scale = 192.0 ** (-0.5)
block_len = 32
neg_large = -1e30


def passed_along(block, axis, distance):
    devices = range(lax.axis_size(axis))
    route = [((i - distance) % len(devices), i) for i in devices]
    return lax.ppermute(block, axis, route)


def cache_state(query_block, cache_row, valid_flags, first_block, last_block):
    query_rows = query_block.shape[0]

    def block_step(block_index, carried):
        running_max, running_sum, weighted = carried
        key_block = lax.dynamic_slice_in_dim(cache_row, block_index * block_len, block_len, 0)
        flag_block = lax.dynamic_slice_in_dim(valid_flags, block_index * block_len, block_len, 0)
        scores = (
            lax.dot_general(
                query_block, key_block, (((1,), (1,)), ((), ())), preferred_element_type=jnp.float32
            )
            * soft_scale
        )
        scores = jnp.where(flag_block[None, :], scores, neg_large)
        new_max = jnp.maximum(running_max, jnp.max(scores, axis=1))
        weights = jnp.exp(scores - new_max[:, None])
        factor = jnp.exp(running_max - new_max)
        running_sum = running_sum * factor + jnp.sum(weights, axis=1)
        values = key_block[:, :LAT]
        weighted = weighted * factor[:, None] + jnp.dot(
            weights.astype(jnp.bfloat16), values, preferred_element_type=jnp.float32
        )
        return (new_max, running_sum, weighted)

    initial = (
        jnp.full((query_rows,), neg_large, jnp.float32),
        jnp.zeros((query_rows,), jnp.float32),
        jnp.zeros((query_rows, LAT), jnp.float32),
    )
    return lax.fori_loop(first_block, last_block, block_step, initial)


def fresh_state(query_block, fresh_keys, head_count):
    scores = (
        lax.dot_general(
            query_block, fresh_keys, (((1,), (1,)), ((), ())), preferred_element_type=jnp.float32
        )
        * soft_scale
    )
    query_step = lax.iota(jnp.int32, query_block.shape[0]) // head_count
    key_step = lax.iota(jnp.int32, fresh_keys.shape[0])
    scores = jnp.where(key_step[None, :] <= query_step[:, None], scores, neg_large)
    row_max = jnp.max(scores, axis=1)
    weights = jnp.exp(scores - row_max[:, None])
    weighted = jnp.dot(
        weights.astype(jnp.bfloat16), fresh_keys[:, :LAT], preferred_element_type=jnp.float32
    )
    return (row_max, jnp.sum(weights, axis=1), weighted)


def merge_states(one_state, two_state):
    max_one, sum_one, acc_one = one_state
    max_two, sum_two, acc_two = two_state
    joint_max = jnp.maximum(max_one, max_two)
    scale_one = jnp.exp(max_one - joint_max)
    scale_two = jnp.exp(max_two - joint_max)
    return (
        joint_max,
        sum_one * scale_one + sum_two * scale_two,
        acc_one * scale_one[:, None] + acc_two * scale_two[:, None],
    )


def guest_state(far_query, far_cache, far_flags):
    valid_flags = far_flags > 0
    valid_count = jnp.sum(far_flags.astype(jnp.float32)).astype(jnp.int32)
    first_valid = jnp.argmax(valid_flags)
    first_block = first_valid // block_len
    last_block = (first_valid + valid_count + block_len - 1) // block_len
    return cache_state(far_query, far_cache, valid_flags, first_block, last_block)


def on_device(
    queries,
    latent_cache,
    new_latent,
    lengths,
    hidden,
    norm_gain,
    routes,
    route_weight,
    gate_weight,
    up_weight,
    down_weight,
):
    step_count, local_rows, head_count, key_width = queries.shape
    context_len = latent_cache.shape[1]
    query_rows = step_count * head_count
    half_axis = lax.axis_size("ep") // 2
    positions = lax.iota(jnp.int32, context_len)
    row_ids = lax.iota(jnp.int32, local_rows)
    block_count = (lengths + block_len - 1) // block_len
    longest = jnp.argmax(lengths)
    long_length = lengths[longest]
    long_cache = lax.dynamic_index_in_dim(latent_cache, longest, 0, keepdims=False)
    long_query = lax.dynamic_index_in_dim(queries, longest, 1, keepdims=False).reshape(
        query_rows, key_width
    )
    returned_state = None
    home_blocks = jnp.where(row_ids == longest, 0, block_count)
    sent_flags = (positions < long_length).astype(jnp.bfloat16)
    far_cache, far_query, far_flags = passed_along(
        (long_cache, long_query, sent_flags), "ep", half_axis
    )
    far_state = guest_state(far_query, far_cache, far_flags)
    returned_state = (
        passed_along(far_state[0].astype(jnp.bfloat16), "ep", half_axis).astype(jnp.float32),
        passed_along(far_state[1].astype(jnp.bfloat16), "ep", half_axis).astype(jnp.float32),
        passed_along(far_state[2].astype(jnp.bfloat16), "ep", half_axis).astype(jnp.float32),
    )
    contexts = []
    for row_index in range(local_rows):
        query_block = queries[:, row_index].reshape(query_rows, key_width)
        current_state = cache_state(
            query_block,
            latent_cache[row_index],
            positions < lengths[row_index],
            0,
            home_blocks[row_index],
        )
        current_state = merge_states(
            current_state, fresh_state(query_block, new_latent[:, row_index], head_count)
        )
        joined = merge_states(current_state, returned_state)
        current_state = jax.tree.map(
            lambda left_part, right_part: jnp.where(longest == row_index, left_part, right_part),
            joined,
            current_state,
        )
        final_max, final_sum, weighted = current_state
        contexts.append(
            (weighted / final_sum[:, None])
            .astype(jnp.bfloat16)
            .reshape(step_count, head_count, LAT)
        )
    attended = jnp.stack(contexts, axis=1)
    hidden_f = hidden.astype(jnp.float32)
    mean_square = jnp.mean(hidden_f * hidden_f, axis=-1, keepdims=True)
    normed = (hidden_f * lax.rsqrt(mean_square + 1e-06) * norm_gain).astype(jnp.bfloat16)
    expert_total = lax.axis_size("ep")
    most_slots = max(2, 3 * local_rows * TOPK // expert_total)
    slot_total = expert_total * most_slots
    model_width = hidden.shape[2]
    gate_local = gate_weight[0]
    up_local = up_weight[0]
    down_local = down_weight[0]
    slot_ids = lax.iota(jnp.int32, slot_total)
    pair_ids = lax.iota(jnp.int32, local_rows * TOPK)
    tokens_now = normed[0]
    route_now = routes[0]
    flat_route = route_now.reshape(-1)
    same_expert = (flat_route[:, None] == flat_route[None, :]) & (
        pair_ids[None, :] < pair_ids[:, None]
    )
    pair_rank = jnp.sum(same_expert.astype(jnp.int32), axis=1)
    pair_slot = flat_route * most_slots + pair_rank
    row_slot = jnp.any(
        pair_slot.reshape(local_rows, TOPK)[None, :, :] == slot_ids[:, None, None], axis=2
    )
    send_buffer = jnp.dot(
        row_slot.astype(jnp.bfloat16), tokens_now, preferred_element_type=jnp.float32
    ).astype(jnp.bfloat16)
    send_buffer = send_buffer.reshape(expert_total, most_slots, model_width)
    arrived = lax.all_to_all(send_buffer, "ep", split_axis=0, concat_axis=0, tiled=True)
    flat_rows = arrived.reshape(-1, model_width)
    gate_part = jnp.dot(flat_rows, gate_local, preferred_element_type=jnp.float32)
    up_part = jnp.dot(flat_rows, up_local, preferred_element_type=jnp.float32)
    hidden_units = (jax.nn.silu(gate_part) * up_part).astype(jnp.bfloat16)
    result = (
        jnp.dot(hidden_units, down_local, preferred_element_type=jnp.float32)
        .astype(jnp.bfloat16)
        .reshape(arrived.shape)
    )
    returned = lax.all_to_all(result, "ep", split_axis=0, concat_axis=0, tiled=True)
    picked = (
        jnp.take(returned.reshape(slot_total, model_width), pair_slot, axis=0)
        .astype(jnp.float32)
        .reshape(local_rows, TOPK, model_width)
    )
    step_mixes = [jnp.sum(picked * route_weight[0][:, :, None], axis=1).astype(jnp.bfloat16)]
    expert_mix = jnp.stack(step_mixes, axis=0)
    return (attended, expert_mix)


def solution(mesh):
    placed = (
        P(None, "ep", None, None),
        P("ep", None, None),
        P(None, "ep", None),
        P("ep"),
        P(None, "ep", None),
        P(),
        P(None, "ep", None),
        P(None, "ep", None),
        P("ep", None, None),
        P("ep", None, None),
        P("ep", None, None),
    )
    return jax.shard_map(
        on_device,
        mesh=mesh,
        in_specs=placed,
        out_specs=(P(None, "ep", None, None), P(None, "ep", None)),
        check_vma=False,
    )
```

profile of v0, /device:TPU:1, one launch (start us, length us, event | category | flops | bytes accessed | tf_op | source)
XLA Modules:
  0.0 273.5 jit_solution(13178700984445499948)
XLA Ops:
  0.6 1.3 iota_reduce_fusion.1
  3.8 2.0 fusion.388
  5.8 1.2 compare_convert_fusion
  7.0 3.7 %collective-permute-start = (bf16[128]{0:T(256)(128)(2,1)}, bf16[128]{0:T(256)(128)(2,1)}, u32[]{:S(2)}, u32[]{:S(2)}) collective-permute-start(bf16[128]{0:T(256)(128)(2,1)} %compare_convert_fusion), channel_id=1, source_target_pairs={{64,0},{65,1},{66,2},{67,3},{68,4},{69,5},{70,6},{71,7},{72,8},{73... | collective-permute-start | bytes 776 | tf_op jit(solution)/shard_map/ppermute | solution.py:18
  10.7 3.2 %fusion.387 = (bf16[1,128,576]{1,2,0:T(8,128)(2,1)}, bf16[1,128,576]{1,2,0:T(8,128)(2,1)}, bf16[1,128,576]{1,2,0:T(8,128)(2,1)}, bf16[1,128,576]{1,2,0:T(8,128)(...) fusion(bf16[16,128,576]{1,2,0:T(8,128)(2,1)} %param.46, ...), kind=kLoop, calls=%fused_computation.676 | loop fusion | bytes 5013508 | tf_op jit(solution)/shard_map/slice | solution.py:136
  14.0 0.8 copy.62
  14.9 0.9 slice_bitcast_fusion
  15.8 2.9 %collective-permute-start.2 = (bf16[64,576]{1,0:T(8,128)(2,1)}, bf16[64,576]{1,0:T(8,128)(2,1)}, u32[]{:S(2)}, u32[]{:S(2)}) collective-permute-start(bf16[64,576]{1,0:T(8,128)(2,1)} %get-tuple-element.1241), channel_id=1, source_target_pairs={{64,0},{65,1},{66,2},{67,3},{68,4},{69,5},{70,6},{71,7},{72,8},{73... | collective-permute-start | bytes 221192 | tf_op jit(solution)/shard_map/ppermute | solution.py:18
  19.5 1.8 convolution_convert_fusion
  21.4 4.1 %reshape.642 = bf16[128,3,3584]{2,1,0:T(4,128)(2,1)} reshape(bf16[384,3584]{1,0:T(8,128)(2,1)S(1)} %convolution_convert_fusion) | data formatting | bytes 5505024 | tf_op jit(solution)/shard_map/reshape | solution.py:183
  25.5 9.8 %all-to-all-start = ((bf16[128,3,3584]{2,1,0:T(4,128)(2,1)}), bf16[128,3,3584]{2,1,0:T(4,128)(2,1)}, u32[]{:S(2)}, u32[]{:S(2)}) async-start(bf16[128,3,3584]{2,1,0:T(4,128)(2,1)} %reshape.642), calls=%async_computation | async-start | bytes 7340032 | tf_op jit(solution)/shard_map/all_to_all | solution.py:184
  40.8 0.7 fusion.182
  42.9 0.7 fusion.180
  44.3 0.7 fusion.191
  48.0 4.2 %while.246 = (s32[]{:T(128)}, f32[64]{0:T(128)S(1)}, f32[64]{0:T(128)S(1)}, f32[64,512]{1,0:T(8,128)S(1)}, s32[]{:T(128)}, /*index=5*/pred[128]{0:T(512)(128)(4,...) while((s32[]{:T(128)}, f32[64]{0:T(128)S(1)}, ...), condition=%wide.region_38.39_spmd, body=%wide.region_35.38_spmd.sunk | while | flops 4536454 | bytes 455919 | solution.py:50
  53.0 5.1 %while.247 = (s32[]{:T(128)}, f32[64]{0:T(128)S(1)}, f32[64]{0:T(128)S(1)}, f32[64,512]{1,0:T(8,128)S(1)}, s32[]{:T(128)}, /*index=5*/pred[128]{0:T(512)(128)(4,...) while((s32[]{:T(128)}, f32[64]{0:T(128)S(1)}, ...), condition=%wide.region_42.43_spmd, body=%wide.region_39.42_spmd.sunk | while | flops 4536454 | bytes 455919 | solution.py:50
  59.0 4.2 %while.248 = (s32[]{:T(128)}, f32[64]{0:T(128)S(1)}, f32[64]{0:T(128)S(1)}, f32[64,512]{1,0:T(8,128)S(1)}, s32[]{:T(128)}, /*index=5*/pred[128]{0:T(512)(128)(4,...) while((s32[]{:T(128)}, f32[64]{0:T(128)S(1)}, ...), condition=%wide.region_46.47_spmd, body=%wide.region_43.46_spmd.sunk | while | flops 4536454 | bytes 455919 | solution.py:50
  64.2 4.3 %while.252 = (s32[]{:T(128)}, f32[64]{0:T(128)S(1)}, f32[64]{0:T(128)S(1)}, f32[64,512]{1,0:T(8,128)S(1)}, s32[]{:T(128)}, /*index=5*/pred[128]{0:T(512)(128)(4,...) while((s32[]{:T(128)}, f32[64]{0:T(128)S(1)}, ...), condition=%wide.region_62.63_spmd, body=%wide.region_59.62_spmd.sunk | while | flops 4536454 | bytes 455919 | solution.py:50
  71.9 5.7 %while.243 = (s32[]{:T(128)}, f32[64]{0:T(128)S(1)}, f32[64]{0:T(128)S(1)}, f32[64,512]{1,0:T(8,128)S(1)}, s32[]{:T(128)}, /*index=5*/pred[128]{0:T(512)(128)(4,...) while((s32[]{:T(128)}, f32[64]{0:T(128)S(1)}, ...), condition=%wide.region_26.27_spmd, body=%wide.region_23.26_spmd.sunk | while | flops 4536454 | bytes 455919 | solution.py:50
  78.5 4.5 %while.244 = (s32[]{:T(128)}, f32[64]{0:T(128)S(1)}, f32[64]{0:T(128)S(1)}, f32[64,512]{1,0:T(8,128)S(1)}, s32[]{:T(128)}, /*index=5*/pred[128]{0:T(512)(128)(4,...) while((s32[]{:T(128)}, f32[64]{0:T(128)S(1)}, ...), condition=%wide.region_30.31_spmd, body=%wide.region_27.30_spmd.sunk | while | flops 4536454 | bytes 455919 | solution.py:50
  83.9 4.2 %while.245 = (s32[]{:T(128)}, f32[64]{0:T(128)S(1)}, f32[64]{0:T(128)S(1)}, f32[64,512]{1,0:T(8,128)S(1)}, s32[]{:T(128)}, /*index=5*/pred[128]{0:T(512)(128)(4,...) while((s32[]{:T(128)}, f32[64]{0:T(128)S(1)}, ...), condition=%wide.region_34.35_spmd, body=%wide.region_31.34_spmd.sunk | while | flops 4536454 | bytes 455919 | solution.py:50
  89.0 4.3 %while.253 = (s32[]{:T(128)}, f32[64]{0:T(128)S(1)}, f32[64]{0:T(128)S(1)}, f32[64,512]{1,0:T(8,128)S(1)}, s32[]{:T(128)}, /*index=5*/pred[128]{0:T(512)(128)(4,...) while((s32[]{:T(128)}, f32[64]{0:T(128)S(1)}, ...), condition=%wide.region_66.67_spmd, body=%wide.region_63.66_spmd.sunk | while | flops 4536454 | bytes 455919 | solution.py:50
  96.7 4.0 %while.240 = (s32[]{:T(128)}, f32[64]{0:T(128)S(1)}, f32[64]{0:T(128)S(1)}, f32[64,512]{1,0:T(8,128)S(1)}, s32[]{:T(128)}, /*index=5*/pred[128]{0:T(512)(128)(4,...) while((s32[]{:T(128)}, f32[64]{0:T(128)S(1)}, ...), condition=%wide.region_14.15_spmd, body=%wide.region_11.14_spmd.sunk | while | flops 4536454 | bytes 455919 | solution.py:50
  101.5 4.2 %while.241 = (s32[]{:T(128)}, f32[64]{0:T(128)S(1)}, f32[64]{0:T(128)S(1)}, f32[64,512]{1,0:T(8,128)S(1)}, s32[]{:T(128)}, /*index=5*/pred[128]{0:T(512)(128)(4,...) while((s32[]{:T(128)}, f32[64]{0:T(128)S(1)}, ...), condition=%wide.region_18.19_spmd, body=%wide.region_15.18_spmd.sunk | while | flops 4536454 | bytes 455919 | solution.py:50
  106.6 4.1 %while.242 = (s32[]{:T(128)}, f32[64]{0:T(128)S(1)}, f32[64]{0:T(128)S(1)}, f32[64,512]{1,0:T(8,128)S(1)}, s32[]{:T(128)}, /*index=5*/pred[128]{0:T(512)(128)(4,...) while((s32[]{:T(128)}, f32[64]{0:T(128)S(1)}, ...), condition=%wide.region_22.23_spmd, body=%wide.region_19.22_spmd.sunk | while | flops 4536454 | bytes 455919 | solution.py:50
  114.9 5.7 %while.238 = (s32[]{:T(128)}, f32[64]{0:T(128)S(1)}, f32[64]{0:T(128)S(1)}, f32[64,512]{1,0:T(8,128)S(1)}, s32[]{:T(128)}, /*index=5*/pred[128]{0:T(512)(128)(4,...) while((s32[]{:T(128)}, f32[64]{0:T(128)S(1)}, ...), condition=%wide.region_4.5_spmd, body=%wide.region_1.4_spmd.sunk | while | flops 4536454 | bytes 455919 | solution.py:50
  121.4 5.4 %while.249 = (s32[]{:T(128)}, f32[64]{0:T(128)S(1)}, f32[64]{0:T(128)S(1)}, f32[64,512]{1,0:T(8,128)S(1)}, s32[]{:T(128)}, /*index=5*/pred[128]{0:T(512)(128)(4,...) while((s32[]{:T(128)}, f32[64]{0:T(128)S(1)}, ...), condition=%wide.region_50.51_spmd, body=%wide.region_47.50_spmd.sunk | while | flops 4536454 | bytes 455919 | solution.py:50
  127.5 3.9 %while.250 = (s32[]{:T(128)}, f32[64]{0:T(128)S(1)}, f32[64]{0:T(128)S(1)}, f32[64,512]{1,0:T(8,128)S(1)}, s32[]{:T(128)}, /*index=5*/pred[128]{0:T(512)(128)(4,...) while((s32[]{:T(128)}, f32[64]{0:T(128)S(1)}, ...), condition=%wide.region_54.55_spmd, body=%wide.region_51.54_spmd.sunk | while | flops 4536454 | bytes 455919 | solution.py:50
  132.3 4.2 %while.251 = (s32[]{:T(128)}, f32[64]{0:T(128)S(1)}, f32[64]{0:T(128)S(1)}, f32[64,512]{1,0:T(8,128)S(1)}, s32[]{:T(128)}, /*index=5*/pred[128]{0:T(512)(128)(4,...) while((s32[]{:T(128)}, f32[64]{0:T(128)S(1)}, ...), condition=%wide.region_58.59_spmd, body=%wide.region_55.58_spmd.sunk | while | flops 4536454 | bytes 455919 | solution.py:50
  139.1 1.2 iota_reduce_fusion
  140.9 1.2 convert_reduce_fusion.1
  145.7 2.2 while.239
  145.8 1.1 fusion.503
  146.9 1.0 convolution_add_fusion.35
  148.1 2.9 %collective-permute-start.5 = (bf16[64]{0:T(256)(128)(2,1)S(1)}, bf16[64]{0:T(256)(128)(2,1)S(1)}, u32[]{:S(2)}, u32[]{:S(2)}) collective-permute-start(bf16[64]{0:T(256)(128)(2,1)S(1)} %convert_element_type.200), channel_id=1, source_target_pairs={{64,0},{65,1},{66,2},{67,3},{68,4},{69,5},{70,6},{71,7},{72,8},{73... | collective-permute-start | bytes 392 | tf_op jit(solution)/shard_map/ppermute | solution.py:18
  152.1 1.1 broadcast_select_fusion.2
  153.2 1.1 broadcast_select_fusion.1
  154.4 1.1 broadcast_select_fusion
  155.5 1.1 broadcast_select_fusion.3
  156.6 0.8 bitcast_dynamic-update-slice_fusion.15
  157.4 0.8 bitcast_dynamic-update-slice_fusion.14
  158.2 0.8 bitcast_dynamic-update-slice_fusion.13
  158.9 0.8 bitcast_dynamic-update-slice_fusion.12
  159.7 7.1 %reshape.643 = bf16[384,3584]{1,0:T(8,128)(2,1)} reshape(bf16[128,3,3584]{2,1,0:T(4,128)(2,1)} %all-to-all-done) | data formatting | bytes 5505024 | tf_op jit(solution)/shard_map/reshape | solution.py:185
  166.7 8.1 %fusion.157 = f32[384,1024]{1,0:T(8,128)} fusion(bf16[384,3584]{1,0:T(8,128)(2,1)} %reshape.643, bf16[1,3584,1024]{2,1,0:T(8,128)(2,1)} %param.53), kind=kOutput, calls=%fused_computation.226 | convolution fusion | flops 2818572288 | bytes 11665408 | tf_op jit(solution)/shard_map/dot_general | solution.py:186
  174.8 13.9 %fusion.159 = bf16[384,3584]{1,0:T(8,128)(2,1)} fusion(bf16[1,1024,3584]{2,1,0:T(8,128)(2,1)} %param.55, f32[384,1024]{1,0:T(8,128)} %fusion.157, bf16[384,3584]{1,0:T(8,128)(2,1)} %reshape.643, bf16[1,3584,1024]{2,1,0:T(8,128)(2,1)} %param.54), kind=kOutput, calls=%fused_computation.229 | convolution fusion | flops 5640880128 | bytes 21757952 | tf_op jit(solution)/shard_map/dot_general | solution.py:190
  188.7 6.7 %reshape.644 = bf16[128,3,3584]{2,1,0:T(4,128)(2,1)} reshape(bf16[384,3584]{1,0:T(8,128)(2,1)} %fusion.159) | data formatting | bytes 5505024 | tf_op jit(solution)/shard_map/reshape | solution.py:192
  195.4 20.7 %all-to-all-start.1 = ((bf16[128,3,3584]{2,1,0:T(4,128)(2,1)}), bf16[128,3,3584]{2,1,0:T(4,128)(2,1)}, u32[]{:S(2)}, u32[]{:S(2)}) async-start(bf16[128,3,3584]{2,1,0:T(4,128)(2,1)} %reshape.644), calls=%async_computation.1 | async-start | bytes 7340032 | tf_op jit(solution)/shard_map/all_to_all | solution.py:194
  216.1 0.8 bitcast_dynamic-update-slice_fusion.11
  216.8 0.8 bitcast_dynamic-update-slice_fusion.10
  217.6 0.8 bitcast_dynamic-update-slice_fusion.9
  218.4 0.8 bitcast_dynamic-update-slice_fusion.8
  219.1 0.8 bitcast_dynamic-update-slice_fusion.7
  219.9 0.8 bitcast_dynamic-update-slice_fusion.6
  220.6 0.8 bitcast_dynamic-update-slice_fusion.5
  221.4 0.8 bitcast_dynamic-update-slice_fusion.4
  222.1 0.8 bitcast_dynamic-update-slice_fusion.3
  222.9 0.8 bitcast_dynamic-update-slice_fusion.2
  223.7 0.8 bitcast_dynamic-update-slice_fusion.1
  224.4 0.8 bitcast_dynamic-update-slice_fusion
  225.2 38.0 %all-to-all-done.1 = bf16[128,3,3584]{2,1,0:T(4,128)(2,1)} async-done(((bf16[128,3,3584]{2,1,0:T(4,128)(2,1)}), bf16[128,3,3584]{2,1,0:T(4,128)(2,1)}, u32[]{:S(2)}, u32[]{:S(2)}) %all-to-all-start.1) | async-done | bytes 2752544 | tf_op jit(solution)/shard_map/all_to_all | solution.py:194
  263.2 5.6 %reshape.645 = bf16[384,3584]{1,0:T(8,128)(2,1)S(1)} reshape(bf16[128,3,3584]{2,1,0:T(4,128)(2,1)} %all-to-all-done.1) | data formatting | bytes 5505024 | tf_op jit(solution)/shard_map/reshape | solution.py:196
  268.9 2.0 gather_fusion
  270.9 2.6 multiply_reduce_fusion
  (601 shorter events, 50.7 us)
Async XLA Ops:
  7.0 7.9 %copy-start.7 = (bf16[1,16,64,576]{3,2,1,0:T(8,128)(2,1)S(1)}, bf16[1,16,64,576]{3,2,1,0:T(8,128)(2,1)}, u32[]{:S(2)}) copy-start(bf16[1,16,64,576]{3,2,1,0:T(8,128)(2,1)} %param.45) | copy-start | bytes 3538948
  7.0 132.1 %collective-permute-start = (bf16[128]{0:T(256)(128)(2,1)}, bf16[128]{0:T(256)(128)(2,1)}, u32[]{:S(2)}, u32[]{:S(2)}) collective-permute-start(bf16[128]{0:T(256)(128)(2,1)} %compare_convert_fusion), channel_id=1, source_target_pairs={{64,0},{65,1},{66,2},{67,3},{68,4},{69,5},{70,6},{71,7},{72,8},{73... | collective-permute-start | bytes 776 | tf_op jit(solution)/shard_map/ppermute | solution.py:18
  13.9 4.7 %copy-start.28 = (s32[1,16,8]{1,2,0:T(8,128)S(1)}, s32[1,16,8]{1,2,0:T(8,128)}, u32[]{:S(2)}) copy-start(s32[1,16,8]{1,2,0:T(8,128)} %param.51) | copy-start | bytes 1540
  14.0 5.4 %copy-start.25 = (bf16[1,16,3584]{2,1,0:T(8,128)(2,1)S(1)}, bf16[1,16,3584]{2,1,0:T(8,128)(2,1)}, u32[]{:S(2)}) copy-start(bf16[1,16,3584]{2,1,0:T(8,128)(2,1)} %param.49) | copy-start | bytes 344068
  14.8 4.8 %copy-start.29 = (f32[3584]{0:T(1024)S(1)}, f32[3584]{0:T(1024)}, u32[]{:S(2)}) copy-start(f32[3584]{0:T(1024)} %param.50) | copy-start | bytes 43012
  14.8 130.7 %collective-permute-start.1 = (bf16[128,576]{1,0:T(8,128)(2,1)}, bf16[128,576]{1,0:T(8,128)(2,1)}, u32[]{:S(2)}, u32[]{:S(2)}) collective-permute-start(bf16[128,576]{1,0:T(8,128)(2,1)} %bitcast.8), channel_id=1, source_target_pairs={{64,0},{65,1},{66,2},{67,3},{68,4},{69,5},{70,6},{71,7},{72,8},{73... | collective-permute-start | bytes 442376 | tf_op jit(solution)/shard_map/ppermute | solution.py:18
  15.8 129.8 %collective-permute-start.2 = (bf16[64,576]{1,0:T(8,128)(2,1)}, bf16[64,576]{1,0:T(8,128)(2,1)}, u32[]{:S(2)}, u32[]{:S(2)}) collective-permute-start(bf16[64,576]{1,0:T(8,128)(2,1)} %get-tuple-element.1241), channel_id=1, source_target_pairs={{64,0},{65,1},{66,2},{67,3},{68,4},{69,5},{70,6},{71,7},{72,8},{73... | collective-permute-start | bytes 221192 | tf_op jit(solution)/shard_map/ppermute | solution.py:18
  19.0 26.7 %copy-start.44 = (s32[128]{0:T(128)}, s32[128]{0:T(128)S(1)}, u32[]{:S(2)}) copy-start(s32[128]{0:T(128)S(1)} %convert_reduce_fusion) | copy-start | bytes 1540
  25.5 9.8 %copy-start.26 = (s32[16]{0:T(128)S(1)}, s32[16]{0:T(128)}, u32[]{:S(2)}) copy-start(s32[16]{0:T(128)} %param.48) | copy-start | bytes 196
  25.5 10.5 %copy-start.8 = (bf16[1,16,64,576]{3,2,1,0:T(8,128)(2,1)S(1)}, bf16[1,16,64,576]{3,2,1,0:T(8,128)(2,1)}, u32[]{:S(2)}) copy-start(bf16[1,16,64,576]{3,2,1,0:T(8,128)(2,1)} %param.45) | copy-start | bytes 3538948
  25.5 10.5 %copy-start.27 = (bf16[1,16,576]{2,1,0:T(8,128)(2,1)S(1)}, bf16[1,16,576]{2,1,0:T(8,128)(2,1)}, u32[]{:S(2)}) copy-start(bf16[1,16,576]{2,1,0:T(8,128)(2,1)} %param.47) | copy-start | bytes 55300
  25.5 134.2 %all-to-all-start = ((bf16[128,3,3584]{2,1,0:T(4,128)(2,1)}), bf16[128,3,3584]{2,1,0:T(4,128)(2,1)}, u32[]{:S(2)}, u32[]{:S(2)}) async-start(bf16[128,3,3584]{2,1,0:T(4,128)(2,1)} %reshape.642), calls=%async_computation | async-start | bytes 7340032 | tf_op jit(solution)/shard_map/all_to_all | solution.py:184
  35.3 10.5 %copy-start.24 = (bf16[1,128,576]{1,2,0:T(8,128)(2,1)S(1)}, bf16[1,128,576]{1,2,0:T(8,128)(2,1)}, u32[]{:S(2)}) copy-start(bf16[1,128,576]{1,2,0:T(8,128)(2,1)} %get-tuple-element.1218) | copy-start | bytes 442372
  35.3 12.7 %copy-start.6 = (bf16[64,576]{1,0:T(8,128)(2,1)S(1)}, bf16[64,576]{1,0:T(8,128)(2,1)}, u32[]{:S(2)}) copy-start(bf16[64,576]{1,0:T(8,128)(2,1)} %get-tuple-element.2892) | copy-start | bytes 221188
  45.8 6.4 %copy-start.23 = (bf16[1,128,576]{1,2,0:T(8,128)(2,1)S(1)}, bf16[1,128,576]{1,2,0:T(8,128)(2,1)}, u32[]{:S(2)}) copy-start(bf16[1,128,576]{1,2,0:T(8,128)(2,1)} %get-tuple-element.1217) | copy-start | bytes 442372
  48.0 5.0 %copy-start.5 = (bf16[64,576]{1,0:T(8,128)(2,1)S(1)}, bf16[64,576]{1,0:T(8,128)(2,1)}, u32[]{:S(2)}) copy-start(bf16[64,576]{1,0:T(8,128)(2,1)} %get-tuple-element.2928) | copy-start | bytes 221188
  52.2 6.0 %copy-start.22 = (bf16[1,128,576]{1,2,0:T(8,128)(2,1)S(1)}, bf16[1,128,576]{1,2,0:T(8,128)(2,1)}, u32[]{:S(2)}) copy-start(bf16[1,128,576]{1,2,0:T(8,128)(2,1)} %get-tuple-element.1216) | copy-start | bytes 442372
  53.0 6.0 %copy-start.4 = (bf16[64,576]{1,0:T(8,128)(2,1)S(1)}, bf16[64,576]{1,0:T(8,128)(2,1)}, u32[]{:S(2)}) copy-start(bf16[64,576]{1,0:T(8,128)(2,1)} %get-tuple-element.2964) | copy-start | bytes 221188
  58.2 5.1 %copy-start.21 = (bf16[1,128,576]{1,2,0:T(8,128)(2,1)S(1)}, bf16[1,128,576]{1,2,0:T(8,128)(2,1)}, u32[]{:S(2)}) copy-start(bf16[1,128,576]{1,2,0:T(8,128)(2,1)} %get-tuple-element.1212) | copy-start | bytes 442372
  59.0 5.2 %copy-start.3 = (bf16[64,576]{1,0:T(8,128)(2,1)S(1)}, bf16[64,576]{1,0:T(8,128)(2,1)}, u32[]{:S(2)}) copy-start(bf16[64,576]{1,0:T(8,128)(2,1)} %get-tuple-element.2856) | copy-start | bytes 221188
  63.3 7.7 %copy-start.20 = (bf16[1,128,576]{1,2,0:T(8,128)(2,1)S(1)}, bf16[1,128,576]{1,2,0:T(8,128)(2,1)}, u32[]{:S(2)}) copy-start(bf16[1,128,576]{1,2,0:T(8,128)(2,1)} %get-tuple-element.1221) | copy-start | bytes 442372
  64.2 7.6 %copy-start.2 = (bf16[64,576]{1,0:T(8,128)(2,1)S(1)}, bf16[64,576]{1,0:T(8,128)(2,1)}, u32[]{:S(2)}) copy-start(bf16[64,576]{1,0:T(8,128)(2,1)} %get-tuple-element.2748) | copy-start | bytes 221188
  71.0 6.6 %copy-start.19 = (bf16[1,128,576]{1,2,0:T(8,128)(2,1)S(1)}, bf16[1,128,576]{1,2,0:T(8,128)(2,1)}, u32[]{:S(2)}) copy-start(bf16[1,128,576]{1,2,0:T(8,128)(2,1)} %get-tuple-element.1220) | copy-start | bytes 442372
  71.9 6.6 %copy-start.1 = (bf16[64,576]{1,0:T(8,128)(2,1)S(1)}, bf16[64,576]{1,0:T(8,128)(2,1)}, u32[]{:S(2)}) copy-start(bf16[64,576]{1,0:T(8,128)(2,1)} %get-tuple-element.2784) | copy-start | bytes 221188
  77.6 5.4 %copy-start.18 = (bf16[1,128,576]{1,2,0:T(8,128)(2,1)S(1)}, bf16[1,128,576]{1,2,0:T(8,128)(2,1)}, u32[]{:S(2)}) copy-start(bf16[1,128,576]{1,2,0:T(8,128)(2,1)} %get-tuple-element.1219) | copy-start | bytes 442372
  78.5 5.4 %copy-start = (bf16[64,576]{1,0:T(8,128)(2,1)S(1)}, bf16[64,576]{1,0:T(8,128)(2,1)}, u32[]{:S(2)}) copy-start(bf16[64,576]{1,0:T(8,128)(2,1)} %get-tuple-element.2820) | copy-start | bytes 221188
  83.0 5.2 %copy-start.17 = (bf16[1,128,576]{1,2,0:T(8,128)(2,1)S(1)}, bf16[1,128,576]{1,2,0:T(8,128)(2,1)}, u32[]{:S(2)}) copy-start(bf16[1,128,576]{1,2,0:T(8,128)(2,1)} %get-tuple-element.1211) | copy-start | bytes 442372
  88.2 7.6 %copy-start.16 = (bf16[1,128,576]{1,2,0:T(8,128)(2,1)S(1)}, bf16[1,128,576]{1,2,0:T(8,128)(2,1)}, u32[]{:S(2)}) copy-start(bf16[1,128,576]{1,2,0:T(8,128)(2,1)} %get-tuple-element.1224) | copy-start | bytes 442372
  93.3 3.4 %copy-start.30 = (f32[64]{0:T(128)}, f32[64]{0:T(128)S(1)}, u32[]{:S(2)}) copy-start(f32[64]{0:T(128)S(1)} %get-tuple-element.817) | copy-start | bytes 772
  95.8 4.9 %copy-start.15 = (bf16[1,128,576]{1,2,0:T(8,128)(2,1)S(1)}, bf16[1,128,576]{1,2,0:T(8,128)(2,1)}, u32[]{:S(2)}) copy-start(bf16[1,128,576]{1,2,0:T(8,128)(2,1)} %get-tuple-element.1223) | copy-start | bytes 442372
  100.7 5.0 %copy-start.14 = (bf16[1,128,576]{1,2,0:T(8,128)(2,1)S(1)}, bf16[1,128,576]{1,2,0:T(8,128)(2,1)}, u32[]{:S(2)}) copy-start(bf16[1,128,576]{1,2,0:T(8,128)(2,1)} %get-tuple-element.1222) | copy-start | bytes 442372
  105.7 5.0 %copy-start.13 = (bf16[1,128,576]{1,2,0:T(8,128)(2,1)S(1)}, bf16[1,128,576]{1,2,0:T(8,128)(2,1)}, u32[]{:S(2)}) copy-start(bf16[1,128,576]{1,2,0:T(8,128)(2,1)} %get-tuple-element.1210) | copy-start | bytes 442372
  114.0 6.6 %copy-start.11 = (bf16[1,128,576]{1,2,0:T(8,128)(2,1)S(1)}, bf16[1,128,576]{1,2,0:T(8,128)(2,1)}, u32[]{:S(2)}) copy-start(bf16[1,128,576]{1,2,0:T(8,128)(2,1)} %get-tuple-element.1215) | copy-start | bytes 442372
  120.6 6.2 %copy-start.10 = (bf16[1,128,576]{1,2,0:T(8,128)(2,1)S(1)}, bf16[1,128,576]{1,2,0:T(8,128)(2,1)}, u32[]{:S(2)}) copy-start(bf16[1,128,576]{1,2,0:T(8,128)(2,1)} %get-tuple-element.1214) | copy-start | bytes 442372
  126.7 4.7 %copy-start.9 = (bf16[1,128,576]{1,2,0:T(8,128)(2,1)S(1)}, bf16[1,128,576]{1,2,0:T(8,128)(2,1)}, u32[]{:S(2)}) copy-start(bf16[1,128,576]{1,2,0:T(8,128)(2,1)} %get-tuple-element.1213) | copy-start | bytes 442372
  131.4 6.5 %copy-start.45 = (s32[128]{0:T(128)S(1)}, s32[128]{0:T(128)}, u32[]{:S(2)}) copy-start(s32[128]{0:T(128)} %copy-done.44) | copy-start | bytes 1540
  131.5 6.6 %copy-start.41 = (bf16[1,576]{1,0:T(2,128)(2,1)S(1)}, bf16[1,576]{1,0:T(2,128)(2,1)}, u32[]{:S(2)}) copy-start(bf16[1,576]{1,0:T(2,128)(2,1)} %get-tuple-element.1245) | copy-start | bytes 3460
  131.5 6.6 %copy-start.42 = (bf16[1,576]{1,0:T(2,128)(2,1)S(1)}, bf16[1,576]{1,0:T(2,128)(2,1)}, u32[]{:S(2)}) copy-start(bf16[1,576]{1,0:T(2,128)(2,1)} %get-tuple-element.1246) | copy-start | bytes 3460
  131.5 6.6 %copy-start.39 = (bf16[1,576]{1,0:T(2,128)(2,1)S(1)}, bf16[1,576]{1,0:T(2,128)(2,1)}, u32[]{:S(2)}) copy-start(bf16[1,576]{1,0:T(2,128)(2,1)} %get-tuple-element.1247) | copy-start | bytes 3460
  131.5 6.6 %copy-start.40 = (bf16[1,576]{1,0:T(2,128)(2,1)S(1)}, bf16[1,576]{1,0:T(2,128)(2,1)}, u32[]{:S(2)}) copy-start(bf16[1,576]{1,0:T(2,128)(2,1)} %get-tuple-element.1248) | copy-start | bytes 3460
  131.5 6.6 %copy-start.37 = (bf16[1,576]{1,0:T(2,128)(2,1)S(1)}, bf16[1,576]{1,0:T(2,128)(2,1)}, u32[]{:S(2)}) copy-start(bf16[1,576]{1,0:T(2,128)(2,1)} %get-tuple-element.1249) | copy-start | bytes 3460
  131.5 6.6 %copy-start.38 = (bf16[1,576]{1,0:T(2,128)(2,1)S(1)}, bf16[1,576]{1,0:T(2,128)(2,1)}, u32[]{:S(2)}) copy-start(bf16[1,576]{1,0:T(2,128)(2,1)} %get-tuple-element.1250) | copy-start | bytes 3460
  131.5 6.6 %copy-start.35 = (bf16[1,576]{1,0:T(2,128)(2,1)S(1)}, bf16[1,576]{1,0:T(2,128)(2,1)}, u32[]{:S(2)}) copy-start(bf16[1,576]{1,0:T(2,128)(2,1)} %get-tuple-element.1251) | copy-start | bytes 3460
  131.5 6.6 %copy-start.36 = (bf16[1,576]{1,0:T(2,128)(2,1)S(1)}, bf16[1,576]{1,0:T(2,128)(2,1)}, u32[]{:S(2)}) copy-start(bf16[1,576]{1,0:T(2,128)(2,1)} %get-tuple-element.1252) | copy-start | bytes 3460
  131.5 6.6 %copy-start.34 = (bf16[1,576]{1,0:T(2,128)(2,1)S(1)}, bf16[1,576]{1,0:T(2,128)(2,1)}, u32[]{:S(2)}) copy-start(bf16[1,576]{1,0:T(2,128)(2,1)} %get-tuple-element.1254) | copy-start | bytes 3460
  131.7 7.3 %copy-start.43 = (f32[1,16,8]{1,2,0:T(8,128)S(1)}, f32[1,16,8]{1,2,0:T(8,128)}, u32[]{:S(2)}) copy-start(f32[1,16,8]{1,2,0:T(8,128)} %param.52) | copy-start | bytes 1540
  138.2 13.8 %copy-start.47 = (f32[64]{0:T(128)S(1)}, f32[64]{0:T(128)}, u32[]{:S(2)}) copy-start(f32[64]{0:T(128)} %fusion.188) | copy-start | bytes 772
  138.2 13.8 %copy-start.49 = (f32[64]{0:T(128)S(1)}, f32[64]{0:T(128)}, u32[]{:S(2)}) copy-start(f32[64]{0:T(128)} %fusion.189) | copy-start | bytes 772
  138.2 13.8 %copy-start.57 = (f32[64]{0:T(128)S(1)}, f32[64]{0:T(128)}, u32[]{:S(2)}) copy-start(f32[64]{0:T(128)} %fusion.187) | copy-start | bytes 772
  145.6 7.6 %copy-start.31 = (f32[64]{0:T(128)S(1)}, f32[64]{0:T(128)}, u32[]{:S(2)}) copy-start(f32[64]{0:T(128)} %copy-done.30) | copy-start | bytes 772
  145.6 7.6 %copy-start.33 = (f32[64]{0:T(128)S(1)}, f32[64]{0:T(128)}, u32[]{:S(2)}) copy-start(f32[64]{0:T(128)} %copy-done.32) | copy-start | bytes 772
  145.6 7.6 %copy-start.54 = (f32[64]{0:T(128)S(1)}, f32[64]{0:T(128)}, u32[]{:S(2)}) copy-start(f32[64]{0:T(128)} %fusion.184) | copy-start | bytes 772
  145.6 7.6 %copy-start.55 = (f32[64]{0:T(128)S(1)}, f32[64]{0:T(128)}, u32[]{:S(2)}) copy-start(f32[64]{0:T(128)} %fusion.185) | copy-start | bytes 772
  145.6 7.6 %copy-start.56 = (f32[64]{0:T(128)S(1)}, f32[64]{0:T(128)}, u32[]{:S(2)}) copy-start(f32[64]{0:T(128)} %fusion.186) | copy-start | bytes 772
  145.6 8.7 %copy-start.48 = (f32[64]{0:T(128)S(1)}, f32[64]{0:T(128)}, u32[]{:S(2)}) copy-start(f32[64]{0:T(128)} %fusion.181) | copy-start | bytes 772
  145.6 8.7 %copy-start.51 = (f32[64]{0:T(128)S(1)}, f32[64]{0:T(128)}, u32[]{:S(2)}) copy-start(f32[64]{0:T(128)} %fusion.182) | copy-start | bytes 772
  145.7 8.7 %copy-start.53 = (f32[64]{0:T(128)S(1)}, f32[64]{0:T(128)}, u32[]{:S(2)}) copy-start(f32[64]{0:T(128)} %fusion.183) | copy-start | bytes 772
  145.7 9.8 %copy-start.46 = (f32[64]{0:T(128)S(1)}, f32[64]{0:T(128)}, u32[]{:S(2)}) copy-start(f32[64]{0:T(128)} %fusion.180) | copy-start | bytes 772
  145.7 9.8 %copy-start.50 = (f32[64]{0:T(128)S(1)}, f32[64]{0:T(128)}, u32[]{:S(2)}) copy-start(f32[64]{0:T(128)} %fusion.190) | copy-start | bytes 772
  145.7 9.8 %copy-start.52 = (f32[64]{0:T(128)S(1)}, f32[64]{0:T(128)}, u32[]{:S(2)}) copy-start(f32[64]{0:T(128)} %fusion.191) | copy-start | bytes 772
  148.0 4.0 %collective-permute-start.3 = (bf16[64]{0:T(256)(128)(2,1)S(1)}, bf16[64]{0:T(256)(128)(2,1)S(1)}, u32[]{:S(2)}, u32[]{:S(2)}) collective-permute-start(bf16[64]{0:T(256)(128)(2,1)S(1)} %convert_element_type.196), channel_id=1, source_target_pairs={{64,0},{65,1},{66,2},{67,3},{68,4},{69,5},{70,6},{71,7},{72,8},{73... | collective-permute-start | bytes 392 | tf_op jit(solution)/shard_map/ppermute | solution.py:18
  148.1 4.0 %collective-permute-start.5 = (bf16[64]{0:T(256)(128)(2,1)S(1)}, bf16[64]{0:T(256)(128)(2,1)S(1)}, u32[]{:S(2)}, u32[]{:S(2)}) collective-permute-start(bf16[64]{0:T(256)(128)(2,1)S(1)} %convert_element_type.200), channel_id=1, source_target_pairs={{64,0},{65,1},{66,2},{67,3},{68,4},{69,5},{70,6},{71,7},{72,8},{73... | collective-permute-start | bytes 392 | tf_op jit(solution)/shard_map/ppermute | solution.py:18
  151.0 5.6 %collective-permute-start.4 = (bf16[64,512]{1,0:T(8,128)(2,1)S(1)}, bf16[64,512]{1,0:T(8,128)(2,1)S(1)}, u32[]{:S(2)}, u32[]{:S(2)}) collective-permute-start(bf16[64,512]{1,0:T(8,128)(2,1)S(1)} %convert_element_type.198), channel_id=1, source_target_pairs={{64,0},{65,1},{66,2},{67,3},{68,4},{69,5},{70,6},{71,7},{72,8},{73... | collective-permute-start | bytes 196616 | tf_op jit(solution)/shard_map/ppermute | solution.py:18
  195.4 67.8 %all-to-all-start.1 = ((bf16[128,3,3584]{2,1,0:T(4,128)(2,1)}), bf16[128,3,3584]{2,1,0:T(4,128)(2,1)}, u32[]{:S(2)}, u32[]{:S(2)}) async-start(bf16[128,3,3584]{2,1,0:T(4,128)(2,1)} %reshape.644), calls=%async_computation.1 | async-start | bytes 7340032 | tf_op jit(solution)/shard_map/all_to_all | solution.py:194
  (2 other events, 6.6 us)
where the time goes:
time: 276 us; the launch traced here: 273 us
  matrix products  57.9 us (21%)
  loops' own time  43.1 us (16%)
  local copies, waits for them, and re-layouts  41.8 us (15%)
  starting transfers between devices  40.6 us (15%)
  waiting for transfers between devices  38.7 us (14%)
  other arithmetic  33.8 us (12%)
  between operations  17.7 us (6%)
    another operation x17, loops' own time, cache_state(): return lax.fori_loop(first_block, last_block, block_step, initial)  43.1 us
    all_to_all x1, waiting for transfers between devices, on_device(): lax.all_to_all(result, 'ep', split_axis=0, concat_axis=0, tiled=True)  38 us
    all_to_all x1, starting transfers between devices, on_device(): lax.all_to_all(result, 'ep', split_axis=0, concat_axis=0, tiled=True)  20.7 us
    dot_general x1, matrix products, on_device(): jnp.dot(hidden_units, down_local, preferred_element_type=jnp.float32)  13.9 us
    dot_general x16, matrix products, fresh_state(): lax.dot_general(query_block, fresh_keys, (((1,), (1,)), ((), ())), prefer...  12.9 us
    dot_general x50, matrix products, block_step(): jnp.dot(weights.astype(jnp.bfloat16), values, preferred_element_type=jnp....  12 us
    unnamed x15, other arithmetic  11.4 us
    ppermute x6, starting transfers between devices, passed_along(): return lax.ppermute(block, axis, route)  10.1 us
  transfers between devices with their start and end apart: 8, of which 3 were waited for; matrix products, arithmetic and copies ran while one was open for 30% of the time, Pallas kernels for 0%

commit v1 on v0

v1 whole, which is shorter than its diff:
```python
import functools

import jax
import jax.numpy as jnp
import numpy as np
from jax import lax
from jax.experimental import pallas as pl
from jax.experimental.pallas import tpu as pltpu
from jax.sharding import PartitionSpec as P

MESH = pl.DeviceIdType.MESH
F32, BF16 = jnp.float32, jnp.bfloat16

D, FF, HEADS, LAT, KDIM, TOPK, CTX, ROWS = 3584, 1024, 64, 512, 576, 8, 128, 16
MOST = 3
SIDE = 4
SLOTS = MOST * SIDE * SIDE
LINE = 2 * SIDE
ALL = SLOTS * LINE
META = 128
soft_scale = 192.0 ** (-0.5)
neg_large = -1e30

PARTS = ((0, 1280, (0, 1, 2)), (1280, 1152, (1, 2, 0)), (2432, 1152, (2, 0, 1)))
STRIDES = (32, 8, 2)


def slot_orders():
    def row(k1, k2, k3, kc, j):
        return (k3 * 2 + kc) * SLOTS + j * SIDE * SIDE + k2 * SIDE + k1

    turns = np.zeros((2, ALL, ALL), np.float32)
    for ky in range(SIDE):
        for kz in range(SIDE):
            for kx in range(SIDE):
                for kc in range(2):
                    for j in range(MOST):
                        k = (ky, kz, kx)
                        rows = [row(k[o[0]], k[o[1]], k[o[2]], kc, j) for _, _, o in PARTS]
                        turns[0, rows[0], rows[1]] = 1
                        turns[1, rows[0], rows[2]] = 1
    return turns


def dot(a, b):
    return jnp.dot(a, b, preferred_element_type=F32)


def dot_t(a, b):
    return lax.dot_general(a, b, (((1,), (1,)), ((), ())), preferred_element_type=F32)


def kernel(
    lengths, fresh, hidden, gain, routes, route_weight, queries, cache, turns, gate_w, up_w, down_w,
    attended, mix,
    q_buf, c_buf, att_buf, turn_buf, wg, wu, wd,
    g1a, g1b, g1c, g2a, g2b, g2c, sa, sb, sc, ra, rb, rc, oa, ob, oc, ca, cb, cc,
    p2a, p2b, p2c, f2a, f2b, f2c, p1a, p1b, p1c, f1a, f1b, f1c,
    pick, mix_hi, mix_lo, tokens, inner,
    local_sem, send_sem, recv_sem,
):
    g1, g2, sel, got, outs, back = (g1a, g1b, g1c), (g2a, g2b, g2c), (sa, sb, sc), (ra, rb, rc), (oa, ob, oc), (ca, cb, cc)
    p2, f2, p1, f1 = (p2a, p2b, p2c), (f2a, f2b, f2c), (p1a, p1b, p1c), (f1a, f1b, f1c)

    me = lax.axis_index("ep")
    place = (me // 32, (me // 8) % 4, (me // 2) % 4)
    core = me % 2

    def device(dim, step, core_step=0):
        moved = (place[dim] + step) % SIDE
        other = (core + core_step) % 2
        return me + (moved - place[dim]) * STRIDES[dim] + (other - core)

    loads = [
        pltpu.make_async_copy(queries.at[0], q_buf, local_sem.at[0]),
        pltpu.make_async_copy(cache, c_buf, local_sem.at[1]),
        pltpu.make_async_copy(gate_w.at[0], wg, local_sem.at[2]),
        pltpu.make_async_copy(up_w.at[0], wu, local_sem.at[3]),
        pltpu.make_async_copy(turns, turn_buf, local_sem.at[4]),
        pltpu.make_async_copy(down_w.at[0], wd, local_sem.at[5]),
    ]
    for load in loads:
        load.start()

    barrier = pltpu.get_barrier_semaphore()
    partners = [device(dim, step, c) for dim in range(3) for step in range(1, SIDE) for c in range(2)]
    partners.append(device(0, 0, 1))
    for partner in partners:
        pl.semaphore_signal(barrier, inc=1, device_id=(partner,), device_id_type=MESH)

    hidden_f = hidden[0].astype(F32)
    mean_square = jnp.mean(hidden_f * hidden_f, axis=-1, keepdims=True)
    normed = (hidden_f * lax.rsqrt(mean_square + 1e-06) * gain[...]).astype(BF16)
    lanes = lax.broadcasted_iota(jnp.int32, (ROWS, META), 1)
    route_now = routes[0]
    weight_now = route_weight[0]
    named = [lanes == route_now[:, k : k + 1] for k in range(TOPK)]
    taken = sum(hit.astype(F32) for hit in named)
    earlier = lax.broadcasted_iota(jnp.int32, (ROWS, ROWS), 0) > lax.broadcasted_iota(jnp.int32, (ROWS, ROWS), 1)
    before = dot(earlier.astype(BF16), taken.astype(BF16))
    meta = jnp.zeros((ROWS, META), F32)
    for k in range(TOPK):
        rank = jnp.sum(jnp.where(named[k], before, 0.0), axis=1, keepdims=True)
        weight = weight_now[:, k : k + 1]
        high = weight.astype(BF16).astype(F32)
        meta = jnp.where(lanes == k, route_now[:, k : k + 1].astype(F32), meta)
        meta = jnp.where(lanes == TOPK + k, rank, meta)
        meta = jnp.where(lanes == 2 * TOPK + k, high, meta)
        meta = jnp.where(lanes == 3 * TOPK + k, weight - high, meta)
    meta = meta.astype(BF16)
    for p, (first, width, _) in enumerate(PARTS):
        g1[p][0:ROWS, 0:width] = normed[:, first : first + width]
        g1[p][0:ROWS, width : width + META] = meta

    pl.semaphore_wait(barrier, len(partners))

    def remote(src, dst, p, number, target):
        return pltpu.make_async_remote_copy(
            src_ref=src, dst_ref=dst, send_sem=send_sem.at[p, number], recv_sem=recv_sem.at[p, number],
            device_id=(target,), device_id_type=MESH,
        )

    def block(ref, number, rows):
        return ref.at[pl.ds(number * rows, rows)]

    first_hops = []
    for p, (_, _, order) in enumerate(PARTS):
        hops = [
            remote(block(g1[p], 0, ROWS), block(g1[p], k, ROWS), p, k - 1, device(order[0], k)) for k in (2, 1, 3)
        ]
        for hop in hops:
            hop.start()
        first_hops.append(hops)

    loads[0].wait()
    loads[1].wait()

    def attend(row, unused):
        q = q_buf[row]
        keys = c_buf[row]
        new = fresh[0]
        scores = dot_t(q, keys) * soft_scale
        scores = jnp.where(lax.broadcasted_iota(jnp.int32, (HEADS, CTX), 1) < lengths[row], scores, neg_large)
        new_scores = dot_t(q, new) * soft_scale
        new_scores = jnp.where(lax.broadcasted_iota(jnp.int32, (HEADS, ROWS), 1) == row, new_scores, neg_large)
        most = jnp.maximum(jnp.max(scores, axis=1, keepdims=True), jnp.max(new_scores, axis=1, keepdims=True))
        weight = jnp.exp(scores - most)
        new_weight = jnp.exp(new_scores - most)
        total = jnp.sum(weight, axis=1, keepdims=True) + jnp.sum(new_weight, axis=1, keepdims=True)
        summed = dot(weight.astype(BF16), keys[:, :LAT]) + dot(new_weight.astype(BF16), new[:, :LAT])
        att_buf[row] = (summed / total).astype(BF16)
        return unused

    lax.fori_loop(0, 4, attend, 0)

    second_hops = []
    for p, (_, _, order) in enumerate(PARTS):
        for hop in first_hops[p]:
            hop.wait_recv()
        g2[p][0:64, :] = g1[p][...]
        hops = [
            remote(block(g2[p], 0, 64), block(g2[p], k, 64), p, 2 + k, device(order[1], k)) for k in (2, 1, 3)
        ]
        for hop in hops:
            hop.start()
        second_hops.append(hops)

    lax.fori_loop(4, 12, attend, 0)

    def targets(p, shape, dim):
        order = PARTS[p][2]
        index = lax.broadcasted_iota(jnp.int32, shape, dim)
        goal = jnp.zeros(shape, jnp.int32)
        for number in range(LINE):
            expert = device(order[2], number // 2, number % 2)
            inside = index - number * SLOTS
            rank = (inside >= 16).astype(jnp.int32) + (inside >= 32).astype(jnp.int32)
            code = (inside - rank * 16) * 512 + expert * 4 + rank
            goal = jnp.where((inside >= 0) & (inside < SLOTS), code, goal)
        return goal.astype(F32)

    third_hops = []
    for p, (_, width, order) in enumerate(PARTS):
        for hop in second_hops[p]:
            hop.wait_recv()
        meta_all = g2[p][:, width : width + META].astype(F32)
        meta_t = jnp.transpose(meta_all)
        home = (lax.broadcasted_iota(jnp.int32, (TOPK, 256), 1) // 16) * 512
        codes = meta_t[0:TOPK] * 4.0 + meta_t[TOPK : 2 * TOPK] + home.astype(F32)
        goal = targets(p, (ALL, 1), 0)
        hit = jnp.zeros((ALL, 256), F32)
        for k in range(TOPK):
            hit = jnp.where(codes[k : k + 1] == goal, 1.0, hit)
        pick[...] = hit.astype(BF16)
        picked = dot(pick[...], g2[p][:, 0:width]).astype(BF16)
        got[p][0:SLOTS, :] = picked[0:SLOTS]
        sel[p][...] = picked[SLOTS:]
        hops = []
        for number in (4, 5, 2, 3, 6, 7, 1):
            hop = remote(
                block(sel[p], number - 1, SLOTS), block(got[p], number, SLOTS), p, 5 + number,
                device(order[2], number // 2, number % 2),
            )
            hop.start()
            hops.append(hop)
        third_hops.append(hops)

    for p, (_, width, order) in enumerate(PARTS):
        meta_all = g2[p][:, width : width + META].astype(F32)
        home = (lax.broadcasted_iota(jnp.int32, (256, 1), 0) // 16) * 512
        goal = targets(p, (1, ALL), 1)
        share = jnp.zeros((256, ALL), F32)
        for k in range(TOPK):
            code = meta_all[:, k : k + 1] * 4.0 + meta_all[:, TOPK + k : TOPK + k + 1] + home.astype(F32)
            weight = meta_all[:, 2 * TOPK + k : 2 * TOPK + k + 1] + meta_all[:, 3 * TOPK + k : 3 * TOPK + k + 1]
            share = jnp.where(code == goal, weight, share)
        high = share.astype(BF16)
        mix_hi[p] = high
        mix_lo[p] = (share - high.astype(F32)).astype(BF16)

    lax.fori_loop(12, ROWS, attend, 0)
    store = pltpu.make_async_copy(att_buf, attended.at[0], local_sem.at[6])
    store.start()

    loads[4].wait()
    for p, (first, width, _) in enumerate(PARTS):
        for hop in third_hops[p]:
            hop.wait_recv()
        rows = got[p][...]
        if p:
            rows = dot(turn_buf[p - 1], rows).astype(BF16)
        tokens[:, first : first + width] = rows
    loads[2].wait()
    loads[3].wait()

    def units(tile, unused):
        columns = pl.ds(pl.multiple_of(tile * 256, 256), 256)
        gate = dot(tokens[...], wg[:, columns])
        up = dot(tokens[...], wu[:, columns])
        inner[:, columns] = (gate / (1.0 + jnp.exp(-gate)) * up).astype(BF16)
        return unused

    lax.fori_loop(0, FF // 256, units, 0)
    loads[5].wait()

    back_hops = []
    for p, (first, width, order) in enumerate(PARTS):
        rows = inner[...]
        if p:
            rows = dot(turn_buf[2 - p], rows).astype(BF16)
        result = dot(rows, wd[:, first : first + width]).astype(BF16)
        back[p][0:SLOTS, :] = result[0:SLOTS]
        outs[p][...] = result[SLOTS:]
        hops = []
        for number in (4, 5, 2, 3, 6, 7, 1):
            hop = remote(
                block(outs[p], number - 1, SLOTS), block(back[p], number, SLOTS), p, 12 + number,
                device(order[2], -(number // 2), number % 2),
            )
            hop.start()
            hops.append(hop)
        back_hops.append(hops)

    late_hops = []
    for p, (_, width, order) in enumerate(PARTS):
        for hop in back_hops[p]:
            hop.wait_recv()
        summed = (dot(mix_hi[p], back[p][...]) + dot(mix_lo[p], back[p][...])).astype(BF16)
        f2[p][0:64, :] = summed[0:64]
        p2[p][...] = summed[64:]
        hops = [
            remote(block(p2[p], k - 1, 64), block(f2[p], k, 64), p, 19 + k, device(order[1], -k)) for k in (2, 1, 3)
        ]
        for hop in hops:
            hop.start()
        late_hops.append(hops)

    last_hops = []
    for p, (_, width, order) in enumerate(PARTS):
        for hop in late_hops[p]:
            hop.wait_recv()
        summed = sum(f2[p][64 * k : 64 * k + 64, :].astype(F32) for k in range(SIDE)).astype(BF16)
        f1[p][0:ROWS, :] = summed[0:ROWS]
        p1[p][...] = summed[ROWS:]
        hops = [
            remote(block(p1[p], k - 1, ROWS), block(f1[p], k, ROWS), p, 22 + k, device(order[0], -k)) for k in (2, 1, 3)
        ]
        for hop in hops:
            hop.start()
        last_hops.append(hops)

    for p, (first, width, _) in enumerate(PARTS):
        for hop in last_hops[p]:
            hop.wait_recv()
        summed = sum(f1[p][ROWS * k : ROWS * k + ROWS, :].astype(F32) for k in range(SIDE))
        mix[0, :, first : first + width] = summed.astype(BF16)

    for hops in first_hops + second_hops + third_hops + back_hops + late_hops + last_hops:
        for hop in hops:
            hop.wait_send()
    store.wait()


def on_device(
    queries, latent_cache, new_latent, lengths, hidden, norm_gain, routes, route_weight, gate_weight, up_weight,
    down_weight,
):
    def per_part(rows, extra=0):
        return [pltpu.VMEM((rows, width + extra), BF16) for _, width, _ in PARTS]

    vmem = pl.BlockSpec(memory_space=pltpu.VMEM)
    smem = pl.BlockSpec(memory_space=pltpu.SMEM)
    hbm = pl.BlockSpec(memory_space=pl.ANY)
    turns = jnp.asarray(slot_orders(), BF16)
    return pl.pallas_call(
        kernel,
        out_shape=(
            jax.ShapeDtypeStruct((1, ROWS, HEADS, LAT), BF16),
            jax.ShapeDtypeStruct((1, ROWS, D), BF16),
        ),
        in_specs=[smem, vmem, vmem, vmem, vmem, vmem] + [hbm] * 6,
        out_specs=(hbm, vmem),
        scratch_shapes=[
            pltpu.VMEM((ROWS, HEADS, KDIM), BF16),
            pltpu.VMEM((ROWS, CTX, KDIM), BF16),
            pltpu.VMEM((ROWS, HEADS, LAT), BF16),
            pltpu.VMEM((2, ALL, ALL), BF16),
            pltpu.VMEM((D, FF), BF16),
            pltpu.VMEM((D, FF), BF16),
            pltpu.VMEM((FF, D), BF16),
            *per_part(64, META),
            *per_part(256, META),
            *per_part(ALL - SLOTS),
            *per_part(ALL),
            *per_part(ALL - SLOTS),
            *per_part(ALL),
            *per_part(192),
            *per_part(256),
            *per_part(48),
            *per_part(64),
            pltpu.VMEM((ALL, 256), BF16),
            pltpu.VMEM((3, 256, ALL), BF16),
            pltpu.VMEM((3, 256, ALL), BF16),
            pltpu.VMEM((ALL, D), BF16),
            pltpu.VMEM((ALL, FF), BF16),
            pltpu.SemaphoreType.DMA((7,)),
            pltpu.SemaphoreType.DMA((3, 26)),
            pltpu.SemaphoreType.DMA((3, 26)),
        ],
        compiler_params=pltpu.CompilerParams(
            collective_id=0, has_side_effects=True, vmem_limit_bytes=61 * 2**20
        ),
    )(
        lengths, new_latent, hidden, norm_gain.reshape(1, D), routes, route_weight, queries, latent_cache, turns,
        gate_weight, up_weight, down_weight,
    )


def solution(mesh):
    placed = (
        P(None, "ep", None, None),
        P("ep", None, None),
        P(None, "ep", None),
        P("ep"),
        P(None, "ep", None),
        P(),
        P(None, "ep", None),
        P(None, "ep", None),
        P("ep", None, None),
        P("ep", None, None),
        P("ep", None, None),
    )
    return jax.shard_map(
        on_device,
        mesh=mesh,
        in_specs=placed,
        out_specs=(P(None, "ep", None, None), P(None, "ep", None)),
        check_vma=False,
    )
```

time: 276 us -> 90.9 us (0.33)
  Pallas kernels: 0 us -> 77.7 us
  matrix products: 57.9 us -> 0 us
  loops' own time: 43.1 us -> 0 us
  starting transfers between devices: 40.6 us -> 0 us
  waiting for transfers between devices: 38.7 us -> 0 us
  other arithmetic: 33.8 us -> 0 us
  local copies, waits for them, and re-layouts: 41.8 us -> 12.2 us
  between operations: 17.7 us -> 0.64 us
    pallas_call x0 -> x1, Pallas kernels: none -> 77.7 us  [on_device(): pl.pallas_call(kernel, out_shape=(jax.ShapeDtypeStruct((1, ROWS, HEADS, L...]
    dot_general x119 -> x0, matrix products: 57.9 us -> none  [the longest x1 13.9 us: on_device(): jnp.dot(hidden_units, down_local, preferred_element_type=jnp.float32)]
    another operation x17 -> x0, loops' own time: 43.1 us -> none  [cache_state(): return lax.fori_loop(first_block, last_block, block_step, initial)]
    all_to_all x2 -> x0, waiting for transfers between devices: 38 us -> none  [the longest x1 38 us: on_device(): lax.all_to_all(result, 'ep', split_axis=0, concat_axis=0, tiled=True)]
    all_to_all x2 -> x0, starting transfers between devices: 30.5 us -> none  [the longest x1 20.7 us: on_device(): lax.all_to_all(result, 'ep', split_axis=0, concat_axis=0, tiled=True)]
    reshape x4 -> x1, local copies, waits for them, and re-layouts: 23.5 us -> 1.33 us  [on_device(): norm_gain.reshape(1, D)]
    unnamed x15 -> x0, other arithmetic: 11.4 us -> none
    ppermute x6 -> x0, starting transfers between devices: 10.1 us -> none  [passed_along(): return lax.ppermute(block, axis, route)]
  transfers between devices with their start and end apart: 8 -> 0, of which waited for: 3 -> 0; matrix products, arithmetic and copies ran while one was open for 30% -> 0% of each run, Pallas kernels for 0% -> 0%
where the time goes in v1:
time: 90.9 us; the launch traced here: 90.5 us
  Pallas kernels  77.7 us (85%)
  local copies, waits for them, and re-layouts  12.2 us (13%)
    pallas_call x1, Pallas kernels, on_device(): pl.pallas_call(kernel, out_shape=(jax.ShapeDtypeStruct((1, ROWS, HEADS, L...  77.7 us
    unnamed x5, local copies, waits for them, and re-layouts  10.9 us

profile of v1, /device:TPU:1, one launch (start us, length us, event | category | flops | bytes accessed | tf_op | source)
XLA Modules:
  0.0 90.5 jit_solution(17177869756206766080)
XLA Ops:
  0.6 1.4 %copy.14.routes = s32[1,16,8]{2,1,0:T(8,128)} copy(s32[1,16,8]{1,2,0:T(8,128)} %param.18) | data formatting | bytes 1024 | tf_op args[6]
  2.0 1.3 %copy.15.route_weight = f32[1,16,8]{2,1,0:T(8,128)} copy(f32[1,16,8]{1,2,0:T(8,128)} %param.19) | data formatting | bytes 1024 | tf_op args[7]
  3.3 1.3 %reshape.7.gain = f32[1,3584]{1,0:T(1,128)} reshape(f32[3584]{0:T(1024)} %param.17) | data formatting | bytes 28672 | tf_op jit(solution)/shard_map/reshape | solution.py:354
  4.7 4.3 %copy.16.cache = bf16[16,128,576]{2,1,0:T(8,128)(2,1)} copy(bf16[16,128,576]{1,2,0:T(8,128)(2,1)} %param.13) | data formatting | bytes 4718592 | tf_op args[1]
  9.0 77.7 %shard_map.131 = (bf16[1,16,64,512]{3,2,1,0:T(8,128)(2,1)}, bf16[1,16,3584]{2,1,0:T(8,128)(2,1)}) custom-call(s32[16]{0:T(128)} %lengths.1, bf16[1,16,576]{2,1,0:T(8,128)(2,1)} %fresh.1, bf16[1,16,3584]{2,1,0:T(8,128)(2,1)} %hidden.1, f32[1,3584]{1,0:T(1,128)} %reshape.7.gain, s32[1,16,8]{2,1,0:T(8,128)} %copy.14.routes, f32[1,16,8]{2,1,0:T(8,128)} %copy.15.route_weight, ...), custom_call_target="tpu_custom_call" | custom-call | tf_op jit(solution)/shard_map/pallas_call | solution.py:315
  86.7 2.3 %copy.19 = bf16[1,16,64,512]{3,2,1,0:T(8,128)(2,1)} copy(bf16[1,16,64,512]{3,2,1,0:T(8,128)(2,1)} %get-tuple-element.4) | data formatting | bytes 2097152
  89.0 1.6 %copy.20 = bf16[1,16,3584]{2,1,0:T(8,128)(2,1)} copy(bf16[1,16,3584]{2,1,0:T(8,128)(2,1)} %get-tuple-element.5) | data formatting | bytes 229376

commit v2 on v1

v2 whole, which is shorter than its diff:
```python
import functools

import jax
import jax.numpy as jnp
import numpy as np
from jax import lax
from jax.experimental import pallas as pl
from jax.experimental.pallas import tpu as pltpu
from jax.sharding import PartitionSpec as P

MESH = pl.DeviceIdType.MESH
F32, BF16 = jnp.float32, jnp.bfloat16

D, FF, HEADS, LAT, KDIM, TOPK, CTX, ROWS = 3584, 1024, 64, 512, 576, 8, 128, 16
MOST = 3
SIDE = 4
SLOTS = MOST * SIDE * SIDE
LINE = 2 * SIDE
ALL = SLOTS * LINE
META = 128
soft_scale = 192.0 ** (-0.5)
neg_large = -1e30

ORDERS = ((0, 1, 2), (1, 2, 0), (2, 0, 1))
PARTS = (
    (0, 640, 0), (640, 640, 1), (1280, 640, 2),
    (1920, 640, 0), (2560, 512, 1), (3072, 512, 2),
)
STRIDES = (32, 8, 2)
HALF = ALL // 2


def slot_orders():
    def row(k1, k2, k3, j):
        return k3 * SLOTS + j * SIDE * SIDE + k2 * SIDE + k1

    turns = np.zeros((2, HALF, HALF), np.float32)
    for ky in range(SIDE):
        for kz in range(SIDE):
            for kx in range(SIDE):
                for j in range(MOST):
                    k = (ky, kz, kx)
                    rows = [row(k[o[0]], k[o[1]], k[o[2]], j) for o in ORDERS]
                    turns[0, rows[0], rows[1]] = 1
                    turns[1, rows[0], rows[2]] = 1
    return turns


def dot(a, b):
    return jnp.dot(a, b, preferred_element_type=F32)


def dot_t(a, b):
    return lax.dot_general(a, b, (((1,), (1,)), ((), ())), preferred_element_type=F32)


def kernel(
    lengths, fresh, hidden, gain, routes, route_weight, queries, cache, turns, gate_w, up_w, down_w,
    attended, mix,
    q_buf, c_buf, att_buf, turn_buf, wg, wu, wd, *rest,
):
    count = len(PARTS)
    g1, g2, sel, got, outs, back, p2, f2, p1, f1, sums = (rest[i * count : (i + 1) * count] for i in range(11))
    pick, mix_hi, mix_lo, tokens, inner, local_sem, send_sem, recv_sem = rest[11 * count :]

    me = lax.axis_index("ep")
    place = (me // 32, (me // 8) % 4, (me // 2) % 4)
    core = me % 2

    def device(dim, step, core_step=0):
        moved = (place[dim] + step) % SIDE
        other = (core + core_step) % 2
        return me + (moved - place[dim]) * STRIDES[dim] + (other - core)

    loads = [
        pltpu.make_async_copy(queries.at[0], q_buf, local_sem.at[0]),
        pltpu.make_async_copy(cache, c_buf, local_sem.at[1]),
        pltpu.make_async_copy(gate_w.at[0], wg, local_sem.at[2]),
        pltpu.make_async_copy(up_w.at[0], wu, local_sem.at[3]),
        pltpu.make_async_copy(turns, turn_buf, local_sem.at[4]),
        pltpu.make_async_copy(down_w.at[0], wd, local_sem.at[5]),
    ]
    for load in loads:
        load.start()

    barrier = pltpu.get_barrier_semaphore()
    partners = [device(dim, step, c) for dim in range(3) for step in range(1, SIDE) for c in range(2)]
    partners.append(device(0, 0, 1))
    for partner in partners:
        pl.semaphore_signal(barrier, inc=1, device_id=(partner,), device_id_type=MESH)

    hidden_f = hidden[0].astype(F32)
    mean_square = jnp.mean(hidden_f * hidden_f, axis=-1, keepdims=True)
    normed = (hidden_f * lax.rsqrt(mean_square + 1e-06) * gain[...].reshape(1, D)).astype(BF16)
    lanes = lax.broadcasted_iota(jnp.int32, (ROWS, META), 1)
    both = jnp.concatenate([routes[0].astype(F32), route_weight[0]], axis=0)
    both = jnp.transpose(both)
    route_now = both[:, 0:TOPK].astype(jnp.int32)
    weight_now = both[:, TOPK : 2 * TOPK]
    named = [lanes == route_now[:, k : k + 1] for k in range(TOPK)]
    taken = sum(hit.astype(F32) for hit in named)
    earlier = lax.broadcasted_iota(jnp.int32, (ROWS, ROWS), 0) > lax.broadcasted_iota(jnp.int32, (ROWS, ROWS), 1)
    before = dot(earlier.astype(BF16), taken.astype(BF16))
    meta = jnp.zeros((ROWS, META), F32)
    for k in range(TOPK):
        rank = jnp.sum(jnp.where(named[k], before, 0.0), axis=1, keepdims=True)
        weight = weight_now[:, k : k + 1]
        high = weight.astype(BF16).astype(F32)
        meta = jnp.where(lanes == k, route_now[:, k : k + 1].astype(F32), meta)
        meta = jnp.where(lanes == TOPK + k, rank, meta)
        meta = jnp.where(lanes == 2 * TOPK + k, high, meta)
        meta = jnp.where(lanes == 3 * TOPK + k, weight - high, meta)
    meta = meta.astype(BF16)
    for p, (first, width, _) in enumerate(PARTS):
        g1[p][0:ROWS, 0:width] = normed[:, first : first + width]
        if p < 3:
            g1[p][0:ROWS, width : width + META] = meta

    pl.semaphore_wait(barrier, len(partners))

    def remote(src, dst, p, number, target):
        return pltpu.make_async_remote_copy(
            src_ref=src, dst_ref=dst, send_sem=send_sem.at[p, number], recv_sem=recv_sem.at[p, number],
            device_id=(target,), device_id_type=MESH,
        )

    def block(ref, number, rows):
        return ref.at[pl.ds(number * rows, rows)]

    first_hops, second_hops = [], []
    for p, (_, _, which) in enumerate(PARTS):
        order = ORDERS[which]
        first_hops.append([
            remote(block(g1[p], 0, ROWS), block(g1[p], k, ROWS), p, k - 1, device(order[0], k)) for k in (2, 1, 3)
        ])
        for hop in first_hops[p]:
            hop.start()
    for p, (_, _, which) in enumerate(PARTS):
        order = ORDERS[which]
        second_hops.append([
            remote(block(g1[p], 0, ROWS), g2[p].at[pl.ds(64 * k, ROWS)], p, 2 + k, device(order[1], k)) for k in (2, 1, 3)
        ])
        for hop in second_hops[p]:
            hop.start()

    loads[0].wait()
    loads[1].wait()

    def attend(row, unused):
        q = q_buf[row]
        keys = c_buf[row]
        new = fresh[0]
        scores = dot(q, keys) * soft_scale
        scores = jnp.where(lax.broadcasted_iota(jnp.int32, (HEADS, CTX), 1) < lengths[row], scores, neg_large)
        new_scores = dot_t(q, new) * soft_scale
        new_scores = jnp.where(lax.broadcasted_iota(jnp.int32, (HEADS, ROWS), 1) == row, new_scores, neg_large)
        most = jnp.maximum(jnp.max(scores, axis=1, keepdims=True), jnp.max(new_scores, axis=1, keepdims=True))
        weight = jnp.exp(scores - most)
        new_weight = jnp.exp(new_scores - most)
        total = jnp.sum(weight, axis=1, keepdims=True) + jnp.sum(new_weight, axis=1, keepdims=True)
        summed = dot_t(weight.astype(BF16), keys[:LAT]) + dot(new_weight.astype(BF16), new[:, :LAT])
        att_buf[row] = (summed / total).astype(BF16)
        return unused

    lax.fori_loop(0, 4, attend, 0)

    for p, (_, _, which) in enumerate(PARTS):
        order = ORDERS[which]
        for hop in first_hops[p]:
            hop.wait_recv()
        hops = [
            remote(
                g1[p].at[pl.ds(ROWS, 48)], g2[p].at[pl.ds(64 * k + ROWS, 48)], p, 5 + k, device(order[1], k)
            ) for k in (2, 1, 3)
        ]
        for hop in hops:
            hop.start()
        second_hops[p] += hops
        g2[p][0:64, :] = g1[p][...]

    lax.fori_loop(4, 12, attend, 0)

    def targets(which, shape, dim):
        index = lax.broadcasted_iota(jnp.int32, shape, dim)
        goal = jnp.zeros(shape, jnp.int32)
        for number in range(LINE):
            expert = device(ORDERS[which][2], number % SIDE, number // SIDE)
            inside = index - number * SLOTS
            rank = (inside >= 16).astype(jnp.int32) + (inside >= 32).astype(jnp.int32)
            code = (inside - rank * 16) * 512 + expert * 4 + rank
            goal = jnp.where((inside >= 0) & (inside < SLOTS), code, goal)
        return goal.astype(F32)

    third_hops = [[[], []] for _ in PARTS]

    def send_picked(p, half):
        order = ORDERS[PARTS[p][2]]
        width = PARTS[p][1]
        picked = dot(pick[p % 3, half * HALF : half * HALF + HALF, :], g2[p][:, 0:width]).astype(BF16)
        if half == 0:
            got[p][0:SLOTS, :] = picked[0:SLOTS]
            sel[p][0 : HALF - SLOTS, :] = picked[SLOTS:]
        else:
            sel[p][HALF - SLOTS :, :] = picked
        for step in (2, 1, 3) if half == 0 else (2, 1, 3, 0):
            number = half * SIDE + step
            hop = remote(
                block(sel[p], number - 1, SLOTS), block(got[p], number, SLOTS), p, 8 + number,
                device(order[2], step, half),
            )
            hop.start()
            third_hops[p][half].append(hop)

    for p, (_, width, which) in enumerate(PARTS):
        for hop in second_hops[p]:
            hop.wait_recv()
        if p < 3:
            meta_t = jnp.transpose(g2[p][:, width : width + META].astype(F32))
            home = (lax.broadcasted_iota(jnp.int32, (TOPK, 256), 1) // 16) * 512
            codes = meta_t[0:TOPK] * 4.0 + meta_t[TOPK : 2 * TOPK] + home.astype(F32)
            goal = targets(which, (ALL, 1), 0)
            hit = jnp.zeros((ALL, 256), F32)
            for k in range(TOPK):
                hit = jnp.where(codes[k : k + 1] == goal, 1.0, hit)
            pick[p] = hit.astype(BF16)
        send_picked(p, 0)
    for p in range(count):
        send_picked(p, 1)

    for p, (_, width, which) in enumerate(PARTS[:3]):
        meta_all = g2[p][:, width : width + META].astype(F32)
        home = (lax.broadcasted_iota(jnp.int32, (256, 1), 0) // 16) * 512
        goal = targets(which, (1, ALL), 1)
        share = jnp.zeros((256, ALL), F32)
        for k in range(TOPK):
            code = meta_all[:, k : k + 1] * 4.0 + meta_all[:, TOPK + k : TOPK + k + 1] + home.astype(F32)
            weight = meta_all[:, 2 * TOPK + k : 2 * TOPK + k + 1] + meta_all[:, 3 * TOPK + k : 3 * TOPK + k + 1]
            share = jnp.where(code == goal, weight, share)
        high = share.astype(BF16)
        low = (share - high.astype(F32)).astype(BF16)
        for half in range(2):
            mix_hi[p, half] = high[:, half * HALF : half * HALF + HALF]
            mix_lo[p, half] = low[:, half * HALF : half * HALF + HALF]

    lax.fori_loop(12, ROWS, attend, 0)
    store = pltpu.make_async_copy(att_buf, attended.at[0], local_sem.at[6])
    store.start()

    loads[4].wait()
    back_hops = [[[], []] for _ in PARTS]
    for half in range(2):
        rows_now = slice(half * HALF, half * HALF + HALF)
        for p, (first, width, which) in enumerate(PARTS):
            for hop in third_hops[p][half]:
                hop.wait_recv()
            rows = got[p][rows_now, :]
            if which:
                rows = dot(turn_buf[which - 1], rows).astype(BF16)
            tokens[:, first : first + width] = rows
        if half == 0:
            loads[2].wait()
            loads[3].wait()

        def units(tile, unused):
            columns = pl.ds(pl.multiple_of(tile * 256, 256), 256)
            gate = dot(tokens[...], wg[:, columns])
            up = dot(tokens[...], wu[:, columns])
            inner[0, :, columns] = (gate / (1.0 + jnp.exp(-gate)) * up).astype(BF16)
            return unused

        lax.fori_loop(0, FF // 256, units, 0)
        if half == 0:
            loads[5].wait()
        for which in (1, 2):
            inner[which] = dot(turn_buf[2 - which], inner[0]).astype(BF16)
        for p, (first, width, which) in enumerate(PARTS):
            order = ORDERS[which]
            result = dot(inner[which], wd[:, first : first + width]).astype(BF16)
            if half == 0:
                back[p][0:SLOTS, :] = result[0:SLOTS]
                outs[p][0 : HALF - SLOTS, :] = result[SLOTS:]
            else:
                outs[p][HALF - SLOTS :, :] = result
            for step in (2, 1, 3) if half == 0 else (2, 1, 3, 0):
                number = half * SIDE + step
                hop = remote(
                    block(outs[p], number - 1, SLOTS), block(back[p], number, SLOTS), p, 16 + number,
                    device(order[2], -step, half),
                )
                hop.start()
                back_hops[p][half].append(hop)

    def relay_sum(p, half):
        for hop in back_hops[p][half]:
            hop.wait_recv()
        rows = back[p][half * HALF : half * HALF + HALF, :]
        return dot(mix_hi[p % 3, half], rows) + dot(mix_lo[p % 3, half], rows)

    for p in range(count):
        sums[p][...] = relay_sum(p, 0)
    late_hops = []
    for p, (_, width, which) in enumerate(PARTS):
        summed = (sums[p][...] + relay_sum(p, 1)).astype(BF16)
        f2[p][0:64, :] = summed[0:64]
        p2[p][...] = summed[64:]
        hops = [
            remote(block(p2[p], k - 1, 64), block(f2[p], k, 64), p, 23 + k, device(ORDERS[which][1], -k))
            for k in (2, 1, 3)
        ]
        for hop in hops:
            hop.start()
        late_hops.append(hops)

    last_hops = []
    for p, (_, width, which) in enumerate(PARTS):
        for hop in late_hops[p]:
            hop.wait_recv()
        summed = sum(f2[p][64 * k : 64 * k + 64, :].astype(F32) for k in range(SIDE)).astype(BF16)
        f1[p][0:ROWS, :] = summed[0:ROWS]
        p1[p][...] = summed[ROWS:]
        hops = [
            remote(block(p1[p], k - 1, ROWS), block(f1[p], k, ROWS), p, 26 + k, device(ORDERS[which][0], -k))
            for k in (2, 1, 3)
        ]
        for hop in hops:
            hop.start()
        last_hops.append(hops)

    for p, (first, width, _) in enumerate(PARTS):
        for hop in last_hops[p]:
            hop.wait_recv()
        summed = sum(f1[p][ROWS * k : ROWS * k + ROWS, :].astype(F32) for k in range(SIDE))
        mix[0, :, first : first + width] = summed.astype(BF16)

    halves = [hops for both in third_hops + back_hops for hops in both]
    for hops in first_hops + second_hops + halves + late_hops + last_hops:
        for hop in hops:
            hop.wait_send()
    store.wait()


def on_device(
    queries, latent_cache, new_latent, lengths, hidden, norm_gain, routes, route_weight, gate_weight, up_weight,
    down_weight,
):
    def per_part(rows, extra=0, dtype=BF16):
        return [
            pltpu.VMEM((rows, width + (extra if p < 3 else 0)), dtype) for p, (_, width, _) in enumerate(PARTS)
        ]

    vmem = pl.BlockSpec(memory_space=pltpu.VMEM)
    smem = pl.BlockSpec(memory_space=pltpu.SMEM)
    hbm = pl.BlockSpec(memory_space=pl.ANY)
    turns = jnp.asarray(slot_orders(), BF16)
    return pl.pallas_call(
        kernel,
        out_shape=(
            jax.ShapeDtypeStruct((1, ROWS, HEADS, LAT), BF16),
            jax.ShapeDtypeStruct((1, ROWS, D), BF16),
        ),
        in_specs=[smem, vmem, vmem, vmem, vmem, vmem] + [hbm] * 6,
        out_specs=(hbm, vmem),
        scratch_shapes=[
            pltpu.VMEM((ROWS, HEADS, KDIM), BF16),
            pltpu.VMEM((ROWS, KDIM, CTX), BF16),
            pltpu.VMEM((ROWS, HEADS, LAT), BF16),
            pltpu.VMEM((2, HALF, HALF), BF16),
            pltpu.VMEM((D, FF), BF16),
            pltpu.VMEM((D, FF), BF16),
            pltpu.VMEM((FF, D), BF16),
            *per_part(64, META),
            *per_part(256, META),
            *per_part(ALL - SLOTS),
            *per_part(ALL),
            *per_part(ALL - SLOTS),
            *per_part(ALL),
            *per_part(192),
            *per_part(256),
            *per_part(48),
            *per_part(64),
            *per_part(256, dtype=F32),
            pltpu.VMEM((3, ALL, 256), BF16),
            pltpu.VMEM((3, 2, 256, HALF), BF16),
            pltpu.VMEM((3, 2, 256, HALF), BF16),
            pltpu.VMEM((HALF, D), BF16),
            pltpu.VMEM((3, HALF, FF), BF16),
            pltpu.SemaphoreType.DMA((7,)),
            pltpu.SemaphoreType.DMA((6, 30)),
            pltpu.SemaphoreType.DMA((6, 30)),
        ],
        compiler_params=pltpu.CompilerParams(
            collective_id=0, has_side_effects=True, vmem_limit_bytes=61 * 2**20
        ),
    )(
        lengths, new_latent, hidden, norm_gain, jnp.swapaxes(routes, 1, 2), jnp.swapaxes(route_weight, 1, 2), queries,
        jnp.swapaxes(latent_cache, 1, 2), turns, gate_weight, up_weight, down_weight,
    )


def solution(mesh):
    placed = (
        P(None, "ep", None, None),
        P("ep", None, None),
        P(None, "ep", None),
        P("ep"),
        P(None, "ep", None),
        P(),
        P(None, "ep", None),
        P(None, "ep", None),
        P("ep", None, None),
        P("ep", None, None),
        P("ep", None, None),
    )
    return jax.shard_map(
        on_device,
        mesh=mesh,
        in_specs=placed,
        out_specs=(P(None, "ep", None, None), P(None, "ep", None)),
        check_vma=False,
    )
```

time: 90.9 us -> 68.9 us (0.76)
  Pallas kernels: 77.7 us -> 64.2 us
  local copies, waits for them, and re-layouts: 12.2 us -> 3.84 us
    pallas_call x1, Pallas kernels: 77.7 us -> 64.2 us  [on_device(): pl.pallas_call(kernel, out_shape=(jax.ShapeDtypeStruct((1, ROWS, HEADS, L...]
    unnamed x5 -> x2, local copies, waits for them, and re-layouts: 10.9 us -> 3.84 us
    reshape x1 -> x0, local copies, waits for them, and re-layouts: 1.33 us -> none  [on_device(): norm_gain.reshape(1, D)]
where the time goes in v2:
time: 68.9 us; the launch traced here: 68.7 us
  Pallas kernels  64.2 us (93%)
  local copies, waits for them, and re-layouts  3.84 us (6%)
    pallas_call x1, Pallas kernels, on_device(): pl.pallas_call(kernel, out_shape=(jax.ShapeDtypeStruct((1, ROWS, HEADS, L...  64.2 us
    unnamed x2, local copies, waits for them, and re-layouts  3.84 us

profile of v2, /device:TPU:1, one launch (start us, length us, event | category | flops | bytes accessed | tf_op | source)
XLA Modules:
  0.0 68.7 jit_solution(7195469920830514140)
XLA Ops:
  0.6 64.2 %shard_map.131 = (bf16[1,16,64,512]{3,2,1,0:T(8,128)(2,1)}, bf16[1,16,3584]{2,1,0:T(8,128)(2,1)}) custom-call(s32[16]{0:T(128)} %lengths.1, bf16[1,16,576]{2,1,0:T(8,128)(2,1)} %fresh.1, bf16[1,16,3584]{2,1,0:T(8,128)(2,1)} %hidden.1, f32[3584]{0:T(1024)} %gain.1, s32[1,8,16]{2,1,0:T(8,128)} %bitcast.4, f32[1,8,16]{2,1,0:T(8,128)} %bitcast.5, ...), custom_call_target="tpu_custom_call" | custom-call | tf_op jit(solution)/shard_map/pallas_call | solution.py:355
  64.8 2.3 %copy.16 = bf16[1,16,64,512]{3,2,1,0:T(8,128)(2,1)} copy(bf16[1,16,64,512]{3,2,1,0:T(8,128)(2,1)} %get-tuple-element.4) | data formatting | bytes 2097152
  67.1 1.6 %copy.17 = bf16[1,16,3584]{2,1,0:T(8,128)(2,1)} copy(bf16[1,16,3584]{2,1,0:T(8,128)(2,1)} %get-tuple-element.5) | data formatting | bytes 229376

commit v3 on v2

v3 whole, which is shorter than its diff:
```python
import functools

import jax
import jax.numpy as jnp
import numpy as np
from jax import lax
from jax.experimental import pallas as pl
from jax.experimental.pallas import tpu as pltpu
from jax.sharding import PartitionSpec as P

MESH = pl.DeviceIdType.MESH
F32, BF16 = jnp.float32, jnp.bfloat16

D, FF, HEADS, LAT, KDIM, TOPK, CTX, ROWS = 3584, 1024, 64, 512, 576, 8, 128, 16
MOST = 3
SIDE = 4
SLOTS = MOST * SIDE * SIDE
LINE = 2 * SIDE
ALL = SLOTS * LINE
META = 128
soft_scale = 192.0 ** (-0.5)
neg_large = -1e30

ORDERS = ((0, 1, 2), (1, 2, 0), (2, 0, 1))
PARTS = ((0, 1280), (1280, 1152), (2432, 1152))
NEAR = 640
STRIDES = (32, 8, 2)
HALF = ALL // 2


def slot_orders():
    def row(k1, k2, k3, j):
        return k3 * SLOTS + j * SIDE * SIDE + k2 * SIDE + k1

    turns = np.zeros((2, HALF, HALF), np.float32)
    for ky in range(SIDE):
        for kz in range(SIDE):
            for kx in range(SIDE):
                for j in range(MOST):
                    k = (ky, kz, kx)
                    rows = [row(k[o[0]], k[o[1]], k[o[2]], j) for o in ORDERS]
                    turns[0, rows[0], rows[1]] = 1
                    turns[1, rows[0], rows[2]] = 1
    return turns


def dot(a, b):
    return jnp.dot(a, b, preferred_element_type=F32)


def dot_t(a, b):
    return lax.dot_general(a, b, (((1,), (1,)), ((), ())), preferred_element_type=F32)


def kernel(
    lengths, fresh, hidden, gain, routes, route_weight, queries, cache, turns, gate_w, up_w, down_w,
    attended, mix,
    q_buf, c_buf, att_buf, turn_buf, wg, wu, wd, *rest,
):
    count = len(PARTS)
    sides = [((0, NEAR), (NEAR, width - NEAR)) for _, width in PARTS]
    g1, g2, sel, got, outs, back, p2, f2, p1, f1, sums = (rest[i * count : (i + 1) * count] for i in range(11))
    pick, mix_hi, mix_lo, tokens, inner, local_sem, send_sem, recv_sem = rest[11 * count :]

    me = lax.axis_index("ep")
    place = (me // 32, (me // 8) % 4, (me // 2) % 4)
    core = me % 2

    def device(dim, step, core_step=0):
        moved = (place[dim] + step) % SIDE
        other = (core + core_step) % 2
        return me + (moved - place[dim]) * STRIDES[dim] + (other - core)

    loads = [
        pltpu.make_async_copy(queries.at[0], q_buf, local_sem.at[0]),
        pltpu.make_async_copy(cache, c_buf, local_sem.at[1]),
        pltpu.make_async_copy(gate_w.at[0], wg, local_sem.at[2]),
        pltpu.make_async_copy(up_w.at[0], wu, local_sem.at[3]),
        pltpu.make_async_copy(turns, turn_buf, local_sem.at[4]),
        pltpu.make_async_copy(down_w.at[0], wd, local_sem.at[5]),
    ]
    for load in loads:
        load.start()

    barrier = pltpu.get_barrier_semaphore()
    partners = [device(dim, step, c) for dim in range(3) for step in range(1, SIDE) for c in range(2)]
    partners.append(device(0, 0, 1))
    for partner in partners:
        pl.semaphore_signal(barrier, inc=1, device_id=(partner,), device_id_type=MESH)

    hidden_f = hidden[0].astype(F32)
    mean_square = jnp.mean(hidden_f * hidden_f, axis=-1, keepdims=True)
    normed = (hidden_f * lax.rsqrt(mean_square + 1e-06) * gain[...].reshape(1, D)).astype(BF16)
    lanes = lax.broadcasted_iota(jnp.int32, (ROWS, META), 1)
    both = jnp.concatenate([routes[0].astype(F32), route_weight[0]], axis=0)
    both = jnp.transpose(both)
    route_now = both[:, 0:TOPK].astype(jnp.int32)
    weight_now = both[:, TOPK : 2 * TOPK]
    named = [lanes == route_now[:, k : k + 1] for k in range(TOPK)]
    taken = sum(hit.astype(F32) for hit in named)
    earlier = lax.broadcasted_iota(jnp.int32, (ROWS, ROWS), 0) > lax.broadcasted_iota(jnp.int32, (ROWS, ROWS), 1)
    before = dot(earlier.astype(BF16), taken.astype(BF16))
    meta = jnp.zeros((ROWS, META), F32)
    for k in range(TOPK):
        rank = jnp.sum(jnp.where(named[k], before, 0.0), axis=1, keepdims=True)
        weight = weight_now[:, k : k + 1]
        high = weight.astype(BF16).astype(F32)
        meta = jnp.where(lanes == k, route_now[:, k : k + 1].astype(F32), meta)
        meta = jnp.where(lanes == TOPK + k, rank, meta)
        meta = jnp.where(lanes == 2 * TOPK + k, high, meta)
        meta = jnp.where(lanes == 3 * TOPK + k, weight - high, meta)
    meta = meta.astype(BF16)
    for p, (first, width) in enumerate(PARTS):
        g1[p][0:ROWS, 0:NEAR] = normed[:, first : first + NEAR]
        g1[p][0:ROWS, NEAR : NEAR + META] = meta
        g1[p][0:ROWS, NEAR + META :] = normed[:, first + NEAR : first + width]

    pl.semaphore_wait(barrier, len(partners))

    def remote(src, dst, p, group, target):
        return pltpu.make_async_remote_copy(
            src_ref=src, dst_ref=dst, send_sem=send_sem.at[p, group], recv_sem=recv_sem.at[p, group],
            device_id=(target,), device_id_type=MESH,
        )

    def landing(p, group):
        width = PARTS[p][1]
        near, far = pl.ds(0, NEAR), pl.ds(NEAR, width - NEAR)
        return (
            g1[p].at[pl.ds(ROWS, 48)], g1[p].at[pl.ds(ROWS, 48)],
            g2[p].at[pl.ds(0, 144), pl.ds(0, NEAR + META)], g2[p].at[pl.ds(0, 144), pl.ds(NEAR + META, width - NEAR)],
            got[p].at[pl.ds(SLOTS, HALF - SLOTS)], got[p].at[pl.ds(HALF, HALF)],
            back[p].at[pl.ds(SLOTS, HALF - SLOTS)],
            back[p].at[pl.ds(HALF, HALF), near], back[p].at[pl.ds(HALF, HALF), far],
            f2[p].at[pl.ds(64, 192), near], f2[p].at[pl.ds(64, 192), far],
            f1[p].at[pl.ds(ROWS, 48)],
        )[group]

    def arrived(p, group):
        remote(landing(p, group), landing(p, group), p, group, device(0, 1)).wait_recv()

    def left(p, group):
        remote(landing(p, group), landing(p, group), p, group, device(0, 1)).wait_send()

    def block(ref, number, rows):
        return ref.at[pl.ds(number * rows, rows)]

    for p in range(count):
        for k in (2, 1, 3):
            remote(block(g1[p], 0, ROWS), block(g1[p], k, ROWS), p, 0, device(ORDERS[p][0], k)).start()
    for p in range(count):
        for k in (2, 1, 3):
            remote(
                block(g1[p], 0, ROWS), g2[p].at[pl.ds(64 * k, ROWS)], p, 1, device(ORDERS[p][1], k)
            ).start()

    loads[0].wait()
    loads[1].wait()

    def attend(row, unused):
        q = q_buf[row]
        keys = c_buf[row]
        new = fresh[0]
        scores = dot(q, keys) * soft_scale
        scores = jnp.where(lax.broadcasted_iota(jnp.int32, (HEADS, CTX), 1) < lengths[row], scores, neg_large)
        new_scores = dot_t(q, new) * soft_scale
        new_scores = jnp.where(lax.broadcasted_iota(jnp.int32, (HEADS, ROWS), 1) == row, new_scores, neg_large)
        most = jnp.maximum(jnp.max(scores, axis=1, keepdims=True), jnp.max(new_scores, axis=1, keepdims=True))
        weight = jnp.exp(scores - most)
        new_weight = jnp.exp(new_scores - most)
        total = jnp.sum(weight, axis=1, keepdims=True) + jnp.sum(new_weight, axis=1, keepdims=True)
        summed = dot_t(weight.astype(BF16), keys[:LAT]) + dot(new_weight.astype(BF16), new[:, :LAT])
        att_buf[row] = (summed / total).astype(BF16)
        return unused

    lax.fori_loop(0, 2, attend, 0)

    for side in range(2):
        for p, (_, width) in enumerate(PARTS):
            if side == 0:
                arrived(p, 0)
            columns = (pl.ds(0, NEAR + META), pl.ds(NEAR + META, width - NEAR))[side]
            for k in (2, 1, 3):
                remote(
                    g1[p].at[pl.ds(ROWS, 48), columns], g2[p].at[pl.ds(64 * k + ROWS, 48), columns],
                    p, 2 + side, device(ORDERS[p][1], k),
                ).start()
    for p in range(count):
        g2[p][0:64, :] = g1[p][...]

    lax.fori_loop(2, 8, attend, 0)

    def targets(p, shape, dim):
        index = lax.broadcasted_iota(jnp.int32, shape, dim)
        goal = jnp.zeros(shape, jnp.int32)
        for number in range(LINE):
            expert = device(ORDERS[p][2], number % SIDE, number // SIDE)
            inside = index - number * SLOTS
            rank = (inside >= 16).astype(jnp.int32) + (inside >= 32).astype(jnp.int32)
            code = (inside - rank * 16) * 512 + expert * 4 + rank
            goal = jnp.where((inside >= 0) & (inside < SLOTS), code, goal)
        return goal.astype(F32)

    def picked(p, half, side):
        first, width = sides[p][side]
        source = first + META * side
        rows = dot(pick[p, half * HALF : half * HALF + HALF, :], g2[p][:, source : source + width]).astype(BF16)
        if half == 0:
            got[p][0:SLOTS, first : first + width] = rows[0:SLOTS]
            sel[p][0 : HALF - SLOTS, first : first + width] = rows[SLOTS:]
        else:
            sel[p][HALF - SLOTS :, first : first + width] = rows

    def send_picked(p, half):
        for step in (2, 1, 3) if half == 0 else (2, 1, 3, 0):
            number = half * SIDE + step
            remote(
                block(sel[p], number - 1, SLOTS), block(got[p], number, SLOTS), p, 4 + half,
                device(ORDERS[p][2], step, half),
            ).start()

    for p in range(count):
        arrived(p, 1)
        arrived(p, 2)
        meta_t = jnp.transpose(g2[p][:, NEAR : NEAR + META].astype(F32))
        home = (lax.broadcasted_iota(jnp.int32, (TOPK, 256), 1) // 16) * 512
        codes = meta_t[0:TOPK] * 4.0 + meta_t[TOPK : 2 * TOPK] + home.astype(F32)
        goal = targets(p, (ALL, 1), 0)
        hit = jnp.zeros((ALL, 256), F32)
        for k in range(TOPK):
            hit = jnp.where(codes[k : k + 1] == goal, 1.0, hit)
        pick[p] = hit.astype(BF16)
        picked(p, 0, 0)
    for p in range(count):
        arrived(p, 3)
        picked(p, 0, 1)
        send_picked(p, 0)
    for p in range(count):
        picked(p, 1, 0)
        picked(p, 1, 1)
        send_picked(p, 1)

    for p in range(count):
        meta_all = g2[p][:, NEAR : NEAR + META].astype(F32)
        home = (lax.broadcasted_iota(jnp.int32, (256, 1), 0) // 16) * 512
        goal = targets(p, (1, ALL), 1)
        share = jnp.zeros((256, ALL), F32)
        for k in range(TOPK):
            code = meta_all[:, k : k + 1] * 4.0 + meta_all[:, TOPK + k : TOPK + k + 1] + home.astype(F32)
            weight = meta_all[:, 2 * TOPK + k : 2 * TOPK + k + 1] + meta_all[:, 3 * TOPK + k : 3 * TOPK + k + 1]
            share = jnp.where(code == goal, weight, share)
        high = share.astype(BF16)
        low = (share - high.astype(F32)).astype(BF16)
        for half in range(2):
            mix_hi[p, half] = high[:, half * HALF : half * HALF + HALF]
            mix_lo[p, half] = low[:, half * HALF : half * HALF + HALF]

    lax.fori_loop(8, 12, attend, 0)

    loads[4].wait()
    def send_back(p, half, columns, group):
        for step in (2, 1, 3) if half == 0 else (2, 1, 3, 0):
            number = half * SIDE + step
            remote(
                outs[p].at[pl.ds((number - 1) * SLOTS, SLOTS), columns],
                back[p].at[pl.ds(number * SLOTS, SLOTS), columns], p, group, device(ORDERS[p][2], -step, half),
            ).start()

    for half in range(2):
        for p, (first, width) in enumerate(PARTS):
            arrived(p, 4 + half)
            rows = got[p][half * HALF : half * HALF + HALF, :]
            if p:
                rows = dot(turn_buf[p - 1], rows).astype(BF16)
            tokens[:, first : first + width] = rows
        if half == 0:
            loads[2].wait()
            loads[3].wait()
        gate = dot(tokens[...], wg[...])
        up = dot(tokens[...], wu[...])
        inner[0] = (gate / (1.0 + jnp.exp(-gate)) * up).astype(BF16)
        if half == 0:
            loads[5].wait()
        for p in (1, 2):
            inner[p] = dot(turn_buf[2 - p], inner[0]).astype(BF16)
        if half == 0:
            for p, (first, width) in enumerate(PARTS):
                result = dot(inner[p], wd[:, first : first + width]).astype(BF16)
                back[p][0:SLOTS, :] = result[0:SLOTS]
                outs[p][0 : HALF - SLOTS, :] = result[SLOTS:]
                send_back(p, 0, pl.ds(0, width), 6)
        else:
            for side in range(2):
                for p, (first, _) in enumerate(PARTS):
                    begin, width = sides[p][side]
                    result = dot(inner[p], wd[:, first + begin : first + begin + width]).astype(BF16)
                    outs[p][HALF - SLOTS :, begin : begin + width] = result
                    send_back(p, 1, pl.ds(begin, width), 7 + side)

    def relay_sum(p, half, begin, width):
        rows = back[p][half * HALF : half * HALF + HALF, begin : begin + width]
        return dot(mix_hi[p, half], rows) + dot(mix_lo[p, half], rows)

    for p, (_, width) in enumerate(PARTS):
        arrived(p, 6)
        sums[p][...] = relay_sum(p, 0, 0, width)
    for side in range(2):
        for p in range(count):
            begin, width = sides[p][side]
            arrived(p, 7 + side)
            columns = slice(begin, begin + width)
            summed = (sums[p][:, columns] + relay_sum(p, 1, begin, width)).astype(BF16)
            f2[p][0:64, columns] = summed[0:64]
            p2[p][:, columns] = summed[64:]
            for k in (2, 1, 3):
                remote(
                    p2[p].at[pl.ds(64 * (k - 1), 64), pl.ds(begin, width)],
                    f2[p].at[pl.ds(64 * k, 64), pl.ds(begin, width)], p, 9 + side, device(ORDERS[p][1], -k),
                ).start()

    lax.fori_loop(12, ROWS, attend, 0)
    store = pltpu.make_async_copy(att_buf, attended.at[0], local_sem.at[6])
    store.start()

    for side in range(2):
        for p in range(count):
            begin, width = sides[p][side]
            arrived(p, 9 + side)
            columns = slice(begin, begin + width)
            summed = sum(f2[p][64 * k : 64 * k + 64, columns].astype(F32) for k in range(SIDE)).astype(BF16)
            f1[p][0:ROWS, columns] = summed[0:ROWS]
            p1[p][:, columns] = summed[ROWS:]
            if side:
                for k in (2, 1, 3):
                    remote(
                        block(p1[p], k - 1, ROWS), block(f1[p], k, ROWS), p, 11, device(ORDERS[p][0], -k)
                    ).start()

    for p, (first, width) in enumerate(PARTS):
        arrived(p, 11)
        summed = sum(f1[p][ROWS * k : ROWS * k + ROWS, :].astype(F32) for k in range(SIDE))
        mix[0, :, first : first + width] = summed.astype(BF16)

    for p in range(count):
        for group in range(12):
            left(p, group)
    store.wait()


def finish(attended, mix, attended_out, mix_out, att_buf, mix_buf, sem):
    pieces, rows = 4, ROWS // 4
    loads = [pltpu.make_async_copy(mix, mix_buf, sem.at[pieces])]
    stores = [pltpu.make_async_copy(mix_buf, mix_out, sem.at[2 * pieces + 1])]
    for i in range(pieces):
        part = pl.ds(i * rows, rows)
        loads.append(pltpu.make_async_copy(attended.at[0, part], att_buf.at[part], sem.at[i]))
        stores.append(pltpu.make_async_copy(att_buf.at[part], attended_out.at[0, part], sem.at[pieces + 1 + i]))
    for load in loads:
        load.start()
    for load, store in zip(loads, stores):
        load.wait()
        store.start()
    for store in stores:
        store.wait()


def on_device(
    queries, latent_cache, new_latent, lengths, hidden, norm_gain, routes, route_weight, gate_weight, up_weight,
    down_weight,
):
    def per_part(rows, extra=0, dtype=BF16):
        return [pltpu.VMEM((rows, width + extra), dtype) for _, width in PARTS]

    vmem = pl.BlockSpec(memory_space=pltpu.VMEM)
    smem = pl.BlockSpec(memory_space=pltpu.SMEM)
    hbm = pl.BlockSpec(memory_space=pl.ANY)
    turns = jnp.asarray(slot_orders(), BF16)
    results = pl.pallas_call(
        kernel,
        out_shape=(
            jax.ShapeDtypeStruct((1, ROWS, HEADS, LAT), BF16),
            jax.ShapeDtypeStruct((1, ROWS, D), BF16),
        ),
        in_specs=[smem, vmem, vmem, vmem, vmem, vmem] + [hbm] * 6,
        out_specs=(hbm, vmem),
        scratch_shapes=[
            pltpu.VMEM((ROWS, HEADS, KDIM), BF16),
            pltpu.VMEM((ROWS, KDIM, CTX), BF16),
            pltpu.VMEM((ROWS, HEADS, LAT), BF16),
            pltpu.VMEM((2, HALF, HALF), BF16),
            pltpu.VMEM((D, FF), BF16),
            pltpu.VMEM((D, FF), BF16),
            pltpu.VMEM((FF, D), BF16),
            *per_part(64, META),
            *per_part(256, META),
            *per_part(ALL - SLOTS),
            *per_part(ALL),
            *per_part(ALL - SLOTS),
            *per_part(ALL),
            *per_part(192),
            *per_part(256),
            *per_part(48),
            *per_part(64),
            *per_part(256, dtype=F32),
            pltpu.VMEM((3, ALL, 256), BF16),
            pltpu.VMEM((3, 2, 256, HALF), BF16),
            pltpu.VMEM((3, 2, 256, HALF), BF16),
            pltpu.VMEM((HALF, D), BF16),
            pltpu.VMEM((3, HALF, FF), BF16),
            pltpu.SemaphoreType.DMA((7,)),
            pltpu.SemaphoreType.DMA((3, 12)),
            pltpu.SemaphoreType.DMA((3, 12)),
        ],
        compiler_params=pltpu.CompilerParams(
            collective_id=0, has_side_effects=True, vmem_limit_bytes=61 * 2**20
        ),
    )(
        lengths, new_latent, hidden, norm_gain, jnp.swapaxes(routes, 1, 2), jnp.swapaxes(route_weight, 1, 2), queries,
        jnp.swapaxes(latent_cache, 1, 2), turns, gate_weight, up_weight, down_weight,
    )
    return pl.pallas_call(
        finish,
        out_shape=(
            jax.ShapeDtypeStruct((1, ROWS, HEADS, LAT), BF16),
            jax.ShapeDtypeStruct((1, ROWS, D), BF16),
        ),
        in_specs=[hbm, hbm],
        out_specs=(hbm, hbm),
        scratch_shapes=[
            pltpu.VMEM((ROWS, HEADS, LAT), BF16),
            pltpu.VMEM((1, ROWS, D), BF16),
            pltpu.SemaphoreType.DMA((10,)),
        ],
    )(*results)


def solution(mesh):
    placed = (
        P(None, "ep", None, None),
        P("ep", None, None),
        P(None, "ep", None),
        P("ep"),
        P(None, "ep", None),
        P(),
        P(None, "ep", None),
        P(None, "ep", None),
        P("ep", None, None),
        P("ep", None, None),
        P("ep", None, None),
    )
    return jax.shard_map(
        on_device,
        mesh=mesh,
        in_specs=placed,
        out_specs=(P(None, "ep", None, None), P(None, "ep", None)),
        check_vma=False,
    )
```

time: 68.9 us -> 63.1 us (0.916)
  local copies, waits for them, and re-layouts: 3.84 us -> 0 us
  Pallas kernels: 64.2 us -> 62.2 us
    pallas_call x1, Pallas kernels: 64.2 us -> 60.1 us  [on_device(): pl.pallas_call(kernel, out_shape=(jax.ShapeDtypeStruct((1, ROWS, HEADS, L...]
    unnamed x2 -> x0, local copies, waits for them, and re-layouts: 3.84 us -> none
    pallas_call x0 -> x1, Pallas kernels: none -> 2.06 us  [on_device(): pl.pallas_call(finish, out_shape=(jax.ShapeDtypeStruct((1, ROWS, HEADS, L...]
where the time goes in v3:
time: 63.1 us; the launch traced here: 63 us
  Pallas kernels  62.2 us (99%)
  between operations  0.8 us (1%)
    pallas_call x1, Pallas kernels, on_device(): pl.pallas_call(kernel, out_shape=(jax.ShapeDtypeStruct((1, ROWS, HEADS, L...  60.1 us
    pallas_call x1, Pallas kernels, on_device(): pl.pallas_call(finish, out_shape=(jax.ShapeDtypeStruct((1, ROWS, HEADS, L...  2.06 us

profile of v3, /device:TPU:1, one launch (start us, length us, event | category | flops | bytes accessed | tf_op | source)
XLA Modules:
  0.0 63.0 jit_solution(8175408684752822468)
XLA Ops:
  0.6 60.1 %shard_map.131 = (bf16[1,16,64,512]{3,2,1,0:T(8,128)(2,1)}, bf16[1,16,3584]{2,1,0:T(8,128)(2,1)}) custom-call(s32[16]{0:T(128)} %lengths.1, bf16[1,16,576]{2,1,0:T(8,128)(2,1)} %fresh.1, bf16[1,16,3584]{2,1,0:T(8,128)(2,1)} %hidden.1, f32[3584]{0:T(1024)} %gain.1, s32[1,8,16]{2,1,0:T(8,128)} %bitcast.4, f32[1,8,16]{2,1,0:T(8,128)} %bitcast.5, ...), custom_call_target="tpu_custom_call" | custom-call | tf_op jit(solution)/shard_map/pallas_call | solution.py:378
  60.7 2.1 %shard_map.132 = (bf16[1,16,64,512]{3,2,1,0:T(8,128)(2,1)}, bf16[1,16,3584]{2,1,0:T(8,128)(2,1)}) custom-call(bf16[1,16,64,512]{3,2,1,0:T(8,128)(2,1)} %get-tuple-element.4.attended, bf16[1,16,3584]{2,1,0:T(8,128)(2,1)} %get-tuple-element.5.mix), custom_call_target="tpu_custom_call" | custom-call | tf_op jit(solution)/shard_map/pallas_call | solution.py:421

commit v4 on v3

--- a/solution.py
+++ b/solution.py
@@ -148,12 +148,6 @@
     for p in range(count):
         for k in (2, 1, 3):
             remote(block(g1[p], 0, ROWS), block(g1[p], k, ROWS), p, 0, device(ORDERS[p][0], k)).start()
-    for p in range(count):
-        for k in (2, 1, 3):
-            remote(
-                block(g1[p], 0, ROWS), g2[p].at[pl.ds(64 * k, ROWS)], p, 1, device(ORDERS[p][1], k)
-            ).start()
-
     loads[0].wait()
     loads[1].wait()
 
@@ -175,6 +169,12 @@
 
     lax.fori_loop(0, 2, attend, 0)
 
+    for p in range(count):
+        for k in (2, 1, 3):
+            remote(
+                block(g1[p], 0, ROWS), g2[p].at[pl.ds(64 * k, ROWS)], p, 1, device(ORDERS[p][1], k)
+            ).start()
+
     for side in range(2):
         for p, (_, width) in enumerate(PARTS):
             if side == 0:
@@ -235,11 +235,6 @@
         arrived(p, 3)
         picked(p, 0, 1)
         send_picked(p, 0)
-    for p in range(count):
-        picked(p, 1, 0)
-        picked(p, 1, 1)
-        send_picked(p, 1)
-
     for p in range(count):
         meta_all = g2[p][:, NEAR : NEAR + META].astype(F32)
         home = (lax.broadcasted_iota(jnp.int32, (256, 1), 0) // 16) * 512
@@ -256,6 +251,12 @@
             mix_lo[p, half] = low[:, half * HALF : half * HALF + HALF]
 
     lax.fori_loop(8, 12, attend, 0)
+
+    for p in range(count):
+        picked(p, 1, 0)
+        picked(p, 1, 1)
+        send_picked(p, 1)
+
 
     loads[4].wait()
     def send_back(p, half, columns, group):

time: 63.1 us -> 61.8 us (0.979)
  Pallas kernels: 62.2 us -> 60.8 us
    pallas_call x1, Pallas kernels: 60.1 us -> 58.8 us  [on_device(): pl.pallas_call(kernel, out_shape=(jax.ShapeDtypeStruct((1, ROWS, HEADS, L...]
where the time goes in v4:
time: 61.8 us; the launch traced here: 61.6 us
  Pallas kernels  60.8 us (98%)
  between operations  0.8 us (1%)
    pallas_call x1, Pallas kernels, on_device(): pl.pallas_call(kernel, out_shape=(jax.ShapeDtypeStruct((1, ROWS, HEADS, L...  58.8 us
    pallas_call x1, Pallas kernels, on_device(): pl.pallas_call(finish, out_shape=(jax.ShapeDtypeStruct((1, ROWS, HEADS, L...  2.06 us

profile of v4, /device:TPU:1, one launch (start us, length us, event | category | flops | bytes accessed | tf_op | source)
XLA Modules:
  0.0 61.6 jit_solution(15886534565460444702)
XLA Ops:
  0.6 58.8 %shard_map.131 = (bf16[1,16,64,512]{3,2,1,0:T(8,128)(2,1)}, bf16[1,16,3584]{2,1,0:T(8,128)(2,1)}) custom-call(s32[16]{0:T(128)} %lengths.1, bf16[1,16,576]{2,1,0:T(8,128)(2,1)} %fresh.1, bf16[1,16,3584]{2,1,0:T(8,128)(2,1)} %hidden.1, f32[3584]{0:T(1024)} %gain.1, s32[1,8,16]{2,1,0:T(8,128)} %bitcast.4, f32[1,8,16]{2,1,0:T(8,128)} %bitcast.5, ...), custom_call_target="tpu_custom_call" | custom-call | tf_op jit(solution)/shard_map/pallas_call | solution.py:379
  59.4 2.1 %shard_map.132 = (bf16[1,16,64,512]{3,2,1,0:T(8,128)(2,1)}, bf16[1,16,3584]{2,1,0:T(8,128)(2,1)}) custom-call(bf16[1,16,64,512]{3,2,1,0:T(8,128)(2,1)} %get-tuple-element.4.attended, bf16[1,16,3584]{2,1,0:T(8,128)(2,1)} %get-tuple-element.5.mix), custom_call_target="tpu_custom_call" | custom-call | tf_op jit(solution)/shard_map/pallas_call | solution.py:422

commit v5 on v4

--- a/solution.py
+++ b/solution.py
@@ -117,9 +117,14 @@
 
     pl.semaphore_wait(barrier, len(partners))
 
+    def departure(p, group):
+        if group < 4:
+            return 3 * min(group, 2) + p
+        return 9 + (0, 1, 2, 3, 3, 4, 4, 5)[group - 4]
+
     def remote(src, dst, p, group, target):
         return pltpu.make_async_remote_copy(
-            src_ref=src, dst_ref=dst, send_sem=send_sem.at[p, group], recv_sem=recv_sem.at[p, group],
+            src_ref=src, dst_ref=dst, send_sem=send_sem.at[departure(p, group)], recv_sem=recv_sem.at[p, group],
             device_id=(target,), device_id_type=MESH,
         )
 
@@ -139,8 +144,8 @@
     def arrived(p, group):
         remote(landing(p, group), landing(p, group), p, group, device(0, 1)).wait_recv()
 
-    def left(p, group):
-        remote(landing(p, group), landing(p, group), p, group, device(0, 1)).wait_send()
+    def left(sent, p, group):
+        remote(sent, sent, p, group, device(0, 1)).wait_send()
 
     def block(ref, number, rows):
         return ref.at[pl.ds(number * rows, rows)]
@@ -343,8 +348,11 @@
         mix[0, :, first : first + width] = summed.astype(BF16)
 
     for p in range(count):
-        for group in range(12):
-            left(p, group)
+        left(landing(p, 0), p, 0)
+        left(landing(p, 1), p, 1)
+        left(g2[p].at[pl.ds(0, 144)], p, 2)
+    for group, rows in ((4, HALF - SLOTS), (5, HALF), (6, HALF - SLOTS), (7, HALF), (9, HALF), (11, 48)):
+        left(tokens.at[pl.ds(0, rows)], 0, group)
     store.wait()
 
 
@@ -409,7 +417,7 @@
             pltpu.VMEM((HALF, D), BF16),
             pltpu.VMEM((3, HALF, FF), BF16),
             pltpu.SemaphoreType.DMA((7,)),
-            pltpu.SemaphoreType.DMA((3, 12)),
+            pltpu.SemaphoreType.DMA((15,)),
             pltpu.SemaphoreType.DMA((3, 12)),
         ],
         compiler_params=pltpu.CompilerParams(

time: 61.8 us -> 61.6 us (level)
  no operation moved by 1% of the time
where the time goes in v5:
time: 61.6 us; the launch traced here: 61.4 us
  Pallas kernels  60.6 us (98%)
  between operations  0.8 us (1%)
    pallas_call x1, Pallas kernels, on_device(): pl.pallas_call(kernel, out_shape=(jax.ShapeDtypeStruct((1, ROWS, HEADS, L...  58.6 us
    pallas_call x1, Pallas kernels, on_device(): pl.pallas_call(finish, out_shape=(jax.ShapeDtypeStruct((1, ROWS, HEADS, L...  2.06 us

profile of v5, /device:TPU:1, one launch (start us, length us, event | category | flops | bytes accessed | tf_op | source)
XLA Modules:
  0.0 61.4 jit_solution(14166985446983873403)
XLA Ops:
  0.6 58.6 %shard_map.131 = (bf16[1,16,64,512]{3,2,1,0:T(8,128)(2,1)}, bf16[1,16,3584]{2,1,0:T(8,128)(2,1)}) custom-call(s32[16]{0:T(128)} %lengths.1, bf16[1,16,576]{2,1,0:T(8,128)(2,1)} %fresh.1, bf16[1,16,3584]{2,1,0:T(8,128)(2,1)} %hidden.1, f32[3584]{0:T(1024)} %gain.1, s32[1,8,16]{2,1,0:T(8,128)} %bitcast.4, f32[1,8,16]{2,1,0:T(8,128)} %bitcast.5, ...), custom_call_target="tpu_custom_call" | custom-call | tf_op jit(solution)/shard_map/pallas_call | solution.py:387
  59.2 2.1 %shard_map.132 = (bf16[1,16,64,512]{3,2,1,0:T(8,128)(2,1)}, bf16[1,16,3584]{2,1,0:T(8,128)(2,1)}) custom-call(bf16[1,16,64,512]{3,2,1,0:T(8,128)(2,1)} %get-tuple-element.4.attended, bf16[1,16,3584]{2,1,0:T(8,128)(2,1)} %get-tuple-element.5.mix), custom_call_target="tpu_custom_call" | custom-call | tf_op jit(solution)/shard_map/pallas_call | solution.py:430
